TPU v7x, 768 devices: a whole 4x8x12 slice. The times are simulated.
768 devices in a mesh: dp: 64 (over y, x, core), mp: 12 (over z).
Axes of the slice: x: 4, y: 8, z: 12, core: 2. Of those that a mesh axis runs over, the one named last changes fastest.
Arguments:
- momentum: float32 [64, 768, 4096], P('dp', 'mp')
- grad: bfloat16 [64, 768, 4096], P('dp', 'mp')
- weights: float32 [768, 4096], P('mp'), may hold values from -6 to 6
- picks: int32 [64, 12, 64, 4], P('dp', 'mp'), may hold values from 0 to 255, as said below
- counts: int32 [64, 12, 64], P('dp', 'mp'), may hold values from 1 to 4, as said below
Outputs:
- new_momentum: float32 [64, 768, 4096], P('dp', 'mp')
- new_weights: float32 [768, 4096], P('mp')
Inputs may be any that keep to these rules, and one draw needn't show every extreme that they name: `picks`: for each replica and group, all 4 entries are distinct block numbers. `counts`: every group has some replica with a count of 4.
All inputs are finite; a program needn't handle non-finite values.
Results may differ from a plain program's by a relative error of at most 0.0004.
Values sent between devices are 32-bit elements; how exact they have to be, the bound alone decides.
No kernel may reach another device: no remote copies, remote signals or barrier semaphores. Data moves between devices by JAX's collectives and lax.ppermute only.
A program may use at most 64 MiB of HBM per device.

v0:
```python
import jax
import jax.numpy as jnp
from jax import lax
from jax.sharding import PartitionSpec as P

GROUP = 64
BLOCK = 4


def basis(size):
    rows = jnp.arange(size, dtype=jnp.float32)[:, None]
    cols = jnp.arange(size, dtype=jnp.float32)[None, :]
    waves = jnp.cos(jnp.pi * (2.0 * cols + 1.0) * rows / (2.0 * size))
    factor = jnp.where(rows == 0.0, jnp.sqrt(1.0 / size), jnp.sqrt(2.0 / size))
    return waves * factor


def inverse(bas, coef):
    width = coef.shape[1] * coef.shape[2]
    right = jnp.einsum("ucv,vn->ucn", coef, bas, precision=lax.Precision.HIGHEST)
    return jnp.dot(bas.T, right.reshape(coef.shape[0], width), precision=lax.Precision.HIGHEST)


def blocks_to_coef(blocks):
    nchunk = blocks.shape[0]
    side = GROUP // BLOCK
    grid = blocks.reshape(nchunk, side, side, BLOCK, BLOCK).transpose(1, 3, 0, 2, 4)
    return grid.reshape(GROUP, nchunk, GROUP)


def on_device(momentum, grad, weights, picks, counts):
    width = weights.shape[1]
    nchunk = width // GROUP
    side = GROUP // BLOCK
    blocks_all = side * side
    replicas = lax.axis_size("dp")
    bas = basis(GROUP)
    moment = 0.9 * momentum[0] + grad[0].astype(jnp.float32)
    left = jnp.dot(bas, moment, precision=lax.Precision.HIGHEST)
    coef = jnp.einsum(
        "ucn,vn->ucv", left.reshape(GROUP, nchunk, GROUP), bas, precision=lax.Precision.HIGHEST
    )
    picked = picks[0, 0]
    block_ids = jnp.arange(blocks_all, dtype=jnp.int32)
    valid = jnp.arange(picked.shape[1], dtype=jnp.int32)[None, :] < counts[0, 0][:, None]
    hits = (picked[..., None] == block_ids) & valid[..., None]
    mask = jnp.any(hits, axis=1).astype(jnp.float32).reshape(nchunk, side, side).transpose(1, 0, 2)
    kept = (coef.reshape(side, BLOCK, nchunk, side, BLOCK) * mask[:, None, :, :, None]).reshape(
        GROUP, nchunk, GROUP
    )
    new_momentum = (moment - inverse(bas, kept))[None]
    blocks = (
        kept.reshape(side, BLOCK, nchunk, side, BLOCK)
        .transpose(2, 0, 3, 1, 4)
        .reshape(nchunk, blocks_all, BLOCK * BLOCK)
    )
    total_rows = GROUP * lax.axis_size("mp") * width
    select = (picked[..., None] == block_ids).astype(jnp.float32)
    values = jnp.einsum("ckb,cbv->ckv", select, blocks, precision=lax.Precision.HIGHEST)
    start_sum = jnp.zeros((nchunk, blocks_all, BLOCK * BLOCK), jnp.float32)
    total = start_sum
    vals_piece = lax.all_gather(values[None], "dp", axis=0, tiled=True)
    picks_piece = lax.all_gather(picked[None], "dp", axis=0, tiled=True)
    for slot in range(vals_piece.shape[2]):
        onehot = (picks_piece[:, :, slot, None] == block_ids).astype(jnp.float32)
        total = total + jnp.einsum(
            "pcb,pcv->cbv", onehot, vals_piece[:, :, slot], precision=lax.Precision.HIGHEST
        )
    update = inverse(bas, blocks_to_coef(total / replicas))
    energy = lax.psum(jnp.sum(update * update), "mp")
    scale = jnp.sqrt(energy / total_rows + 1e-06)
    new_weights = weights - 0.5 * update / scale
    return (new_momentum, new_weights)


def solution(mesh):
    in_specs = (
        P("dp", "mp", None),
        P("dp", "mp", None),
        P("mp", None),
        P("dp", "mp", None, None),
        P("dp", "mp", None),
    )
    out_specs = (P("dp", "mp", None), P("mp", None))
    return jax.shard_map(
        on_device, mesh=mesh, in_specs=in_specs, out_specs=out_specs, check_vma=False
    )
```

profile of v0, /device:TPU:8, one launch (start us, length us, event | category | flops | bytes accessed | tf_op | source)
XLA Modules:
  0.0 217.2 jit_solution(16238641902448022115)
XLA Ops:
  7.2 0.0 all-gather.4.cloned.1.call-start
  7.2 1.5 fusion.17
  8.7 0.6 copy.70
  9.3 6.1 %fusion.30 = f32[64,64,64]{2,0,1:T(8,128)S(1)} fusion(f32[64,64,64]{2,1,0:T(8,128)S(1)} %bitcast.54, f32[64]{0:T(128)S(1)} %get-tuple-element.12, f32[64]{0:T(128)S(1)} %get-tuple-element.13), kind=kOutput, calls=%fused_computation.40 | convolution fusion | flops 201338880 | bytes 2097664 | tf_op jit(solution)/shard_map/dot_general | solution.py:39
  15.5 0.0 copy-start.5
  15.5 3.3 %fusion.5 = f32[64,64,64]{2,1,0:T(8,128)S(1)} fusion(f32[64,64,64]{2,0,1:T(8,128)S(1)} %fusion.30, f32[64]{0:T(128)S(1)} %get-tuple-element.12, f32[64]{0:T(128)S(1)} %get-tuple-element.13), kind=kOutput, calls=%fused_computation.10 | convolution fusion | flops 201338880 | bytes 2097664 | tf_op jit(solution)/shard_map/ucn,vn->ucv/dot_general | solution.py:40
  18.8 0.0 copy-done.4
  18.8 0.1 copy.51
  18.9 0.1 iota_compare_fusion.18
  19.0 0.3 fusion.24
  19.3 0.1 copy.52
  19.4 2.0 copy.55
  21.4 2.1 multiply_bitcast_fusion
  23.5 1.6 copy.56
  25.1 2.5 %copy.57 = f32[64,256,16]{1,2,0:T(8,128)S(1)} copy(f32[64,256,16]{0,1,2:T(8,128)} %bitcast.57) | data formatting | bytes 2097152 | tf_op jit(solution)/shard_map/reshape | solution.py:55
  27.5 1.3 fusion.22
  28.9 0.0 all-gather.4.cloned.1.call-update
  28.9 1.8 mul.153
  30.7 2.9 %copy.53 = f32[64,64,64]{2,1,0:T(8,128)} copy(f32[64,64,64]{1,2,0:T(8,128)} %bitcast.58) | data formatting | bytes 2097152 | tf_op jit(solution)/shard_map/mul | solution.py:48
  33.6 4.8 %fusion.11 = f32[64,64,64]{2,1,0:T(8,128)} fusion(f32[64,64,64]{2,1,0:T(8,128)S(1)} %fusion.5, f32[64,64,64]{2,1,0:T(8,128)} %copy.53, f32[64]{0:T(128)S(1)} %get-tuple-element.12, f32[64]{0:T(128)S(1)} %get-tuple-element.13), kind=kOutput, calls=%fused_computation.17 | convolution fusion | flops 201601024 | bytes 3146240 | tf_op jit(solution)/shard_map/ucv,vn->ucn/dot_general | solution.py:20
  38.4 2.2 %reshape.76 = f32[64,4096]{1,0:T(8,128)S(1)} reshape(f32[64,64,64]{2,1,0:T(8,128)} %fusion.11) | data formatting | bytes 2097152 | tf_op jit(solution)/shard_map/reshape | solution.py:21
  40.7 55.8 %all-gather = s32[64,1,64,4]{2,3,1,0:T(4,128)S(1)} all-gather(s32[1,1,64,4]{2,3,1,0:T(4,128)S(1)} %copy-done.4), channel_id=2, replica_groups=mesh['dp'=64,'mp'=12] {'dp'}, dimensions={0}, use_global_device_ids=true | all-gather | bytes 66560 | tf_op jit(solution)/shard_map/all_gather | solution.py:63
  96.5 0.1 fusion.58
  96.6 0.1 copy.54
  96.7 0.1 copy.60
  96.8 0.1 copy.62
  96.9 0.1 copy.64
  96.9 0.0 copy-done
  97.0 2.2 fusion
  99.1 30.5 %all-gather.4.cloned.1.call-done = f32[4096,4,16]{2,1,0:T(4,128)} async-done(((f32[64,4,16]{2,1,0:T(4,128)}), f32[4096,4,16]{2,1,0:T(4,128)}) %all-gather.4.cloned.1.call-update) | async-done | bytes 1048592 | tf_op jit(solution)/shard_map/all_gather | solution.py:62
  129.6 20.4 %fusion.57 = (f32[64,64,1,16]{3,2,1,0:T(1,128)S(1)}, f32[64,64,1,16]{3,2,1,0:T(1,128)}, f32[64,64,1,16]{3,2,1,0:T(1,128)}, f32[64,64,1,16]{3,2,1,0:T(1,128)}) fusion(f32[64,64,4,16]{3,2,1,0:T(4,128)} %bitcast.56), kind=kLoop, calls=%fused_computation.71 | loop fusion | bytes 2097152 | tf_op jit(solution)/shard_map/slice | solution.py:67
  150.1 4.8 %copy.76 = f32[64,64,1,16]{0,3,1,2:T(8,128)} copy(f32[64,64,1,16]{3,2,1,0:T(1,128)} %get-tuple-element.5) | data formatting | bytes 524288
  154.9 3.8 %copy.77 = f32[64,64,1,16]{0,3,1,2:T(8,128)S(1)} copy(f32[64,64,1,16]{3,2,1,0:T(1,128)} %get-tuple-element.4) | data formatting | bytes 524288
  158.6 3.8 %copy.78 = f32[64,64,1,16]{0,3,1,2:T(8,128)S(1)} copy(f32[64,64,1,16]{3,2,1,0:T(1,128)} %get-tuple-element.3) | data formatting | bytes 524288
  162.4 2.9 %copy.79 = f32[64,64,1,16]{0,3,1,2:T(8,128)} copy(f32[64,64,1,16]{3,2,1,0:T(1,128)S(1)} %get-tuple-element.2) | data formatting | bytes 524288
  165.3 2.7 %fusion.1 = f32[64,256,16]{1,2,0:T(8,128)S(1)} fusion(s32[64,64]{0,1:T(8,128)S(1)} %copy.54, f32[64,64,1,16]{0,3,1,2:T(8,128)} %copy.76), kind=kOutput, calls=%fused_computation.6 | convolution fusion | flops 202375168 | bytes 1327104 | tf_op jit(solution)/shard_map/pcb,pcv->cbv/dot_general | solution.py:66
  168.0 0.0 copy-start.2
  168.0 2.1 fusion.16
  170.1 2.1 fusion.15
  172.2 2.3 %fusion.14 = f32[64,256,16]{1,2,0:T(8,128)S(1)} fusion(f32[64,256,16]{1,2,0:T(8,128)S(1)} %fusion.15, s32[64,64]{0,1:T(8,128)S(1)} %copy.64, f32[64,64,1,16]{0,3,1,2:T(8,128)S(1)} %copy-done.2), kind=kOutput, calls=%fused_computation.20 | convolution fusion | flops 202899456 | bytes 2375680 | tf_op jit(solution)/shard_map/pcb,pcv->cbv/dot_general | solution.py:66
  174.5 0.7 copy.66
  175.2 1.4 copy.67
  176.6 3.5 %fusion.26 = f32[64,64,64]{2,1,0:T(8,128)S(1)} fusion(f32[64,64,64]{1,2,0:T(8,128)S(1)} %bitcast.55, f32[64]{0:T(128)S(1)} %get-tuple-element.12, f32[64]{0:T(128)S(1)} %get-tuple-element.13), kind=kOutput, calls=%fused_computation.36 | convolution fusion | flops 201338880 | bytes 2097664 | tf_op jit(solution)/shard_map/ucv,vn->ucn/dot_general | solution.py:20
  180.1 0.7 reshape.81
  180.7 0.0 copy-start.3
  180.8 1.9 multiply_reduce_fusion
  182.6 25.9 %psum.7 = f32[]{:T(128)} all-reduce(f32[]{:T(128)} %get-tuple-element.10), channel_id=1, replica_groups=mesh['dp'=64,'mp'=12] {'mp'}, use_global_device_ids=true, to_apply=%region_2.3 | all-reduce | flops 1 | bytes 8 | tf_op jit(solution)/shard_map/psum | solution.py:70
  209.2 1.1 divide_subtract_fusion
  (9 shorter events, 0.0 us)
Async XLA Ops:
  7.2 122.5 %all-gather.4.cloned.1.call-start = ((), (), s32[]{:S(2)}) async-start(), calls=%async_computation | async-start | bytes 8519680 | tf_op jit(solution)/shard_map/all_gather | solution.py:62
  15.5 3.3 %copy-start.4 = (s32[1,1,64,4]{2,3,1,0:T(4,128)S(1)}, s32[1,1,64,4]{2,3,1,0:T(4,128)}, u32[]{:S(2)}) copy-start(s32[1,1,64,4]{2,3,1,0:T(4,128)} %param.8) | copy-start | bytes 3076
  15.5 3.4 %copy-start.5 = (s32[1,1,64]{2,1,0:T(1,128)S(1)}, s32[1,1,64]{2,1,0:T(1,128)}, u32[]{:S(2)}) copy-start(s32[1,1,64]{2,1,0:T(1,128)} %param.9) | copy-start | bytes 772
  38.4 58.5 %copy-start = (f32[1,64,4096]{2,1,0:T(8,128)S(1)}, f32[1,64,4096]{2,1,0:T(8,128)}, u32[]{:S(2)}) copy-start(f32[1,64,4096]{2,1,0:T(8,128)} %param.5) | copy-start | bytes 3145732
  38.4 58.5 %copy-start.1 = (bf16[1,64,4096]{2,1,0:T(8,128)(2,1)S(1)}, bf16[1,64,4096]{2,1,0:T(8,128)(2,1)}, u32[]{:S(2)}) copy-start(bf16[1,64,4096]{2,1,0:T(8,128)(2,1)} %param.6) | copy-start | bytes 1572868
  168.0 4.2 %copy-start.2 = (f32[64,64,1,16]{0,3,1,2:T(8,128)S(1)}, f32[64,64,1,16]{0,3,1,2:T(8,128)}, u32[]{:S(2)}) copy-start(f32[64,64,1,16]{0,3,1,2:T(8,128)} %copy.79) | copy-start | bytes 786436
  180.7 28.5 %copy-start.3 = (f32[64,4096]{1,0:T(8,128)S(1)}, f32[64,4096]{1,0:T(8,128)}, u32[]{:S(2)}) copy-start(f32[64,4096]{1,0:T(8,128)} %param.7) | copy-start | bytes 3145732
Sparse Core Ops, SparseCore 0:
  29.0 100.5 all-gather.3
where the time goes:
time: 218 us; the launch traced here: 217 us
  blocking collectives  81.7 us (37%)
  local copies, waits for them, and re-layouts  52.6 us (24%)
  matrix products  32.3 us (15%)
  waiting for transfers between devices  30.5 us (14%)
  between operations  14.9 us (7%)
  other arithmetic  5.02 us (2%)
    all_gather x1, blocking collectives, on_device(): picks_piece = lax.all_gather(picked[None], 'dp', axis=0, tiled=True)  55.8 us
    all_gather x1, waiting for transfers between devices, on_device(): vals_piece = lax.all_gather(values[None], 'dp', axis=0, tiled=True)  30.5 us
    psum x1, blocking collectives, on_device(): energy = lax.psum(jnp.sum(update * update), 'mp')  25.9 us
    slice x1, local copies, waits for them, and re-layouts, on_device(): vals_piece[:, :, slot]  20.4 us
    unnamed x16, local copies, waits for them, and re-layouts  15.3 us
    dot_general x4, matrix products, on_device(): jnp.einsum('pcb,pcv->cbv', onehot, vals_piece[:, :, slot], precision=lax....  9.15 us
    dot_general x2, matrix products, inverse(): jnp.einsum('ucv,vn->ucn', coef, bas, precision=lax.Precision.HIGHEST)  8.34 us
    dot_general x1, matrix products, on_device(): left = jnp.dot(bas, moment, precision=lax.Precision.HIGHEST)  6.15 us
  transfers between devices with their start and end apart: 1, of which 1 were waited for; matrix products, arithmetic and copies ran while one was open for 7% of the time, Pallas kernels for 0%

commit v1 on v0

v1 whole, which is shorter than its diff:
```python
import functools

import jax
import jax.numpy as jnp
import ml_dtypes
import numpy as np
from jax import lax
from jax.experimental import pallas as pl
from jax.experimental.pallas import tpu as pltpu
from jax.sharding import PartitionSpec as P

GROUP = 64
BLOCK = 4
KMAX = 4
SIDE = GROUP // BLOCK
QUAD = 4 * GROUP
ROWS = 40
F32 = jnp.float32
BF16 = jnp.bfloat16
PARAMS = pltpu.CompilerParams(vmem_limit_bytes=48 * 1024 * 1024)


def basis():
    rows = np.arange(GROUP, dtype=np.float64)[:, None]
    cols = np.arange(GROUP, dtype=np.float64)[None, :]
    waves = np.cos(np.pi * (2.0 * cols + 1.0) * rows / (2.0 * GROUP))
    factor = np.where(rows == 0.0, np.sqrt(1.0 / GROUP), np.sqrt(2.0 / GROUP))
    return (waves * factor).astype(np.float32)


def halves(mat):
    high = mat.astype(ml_dtypes.bfloat16)
    low = (mat - high.astype(np.float32)).astype(ml_dtypes.bfloat16)
    return high, low


def left_weights(mat):
    high, low = halves(mat)
    return np.concatenate([high, high, low, low], axis=1)


def right_weights(mat):
    return np.stack(halves(np.kron(np.eye(4, dtype=np.float32), mat)))


def scatter_weights(mat):
    perm = np.arange(GROUP).reshape(SIDE, BLOCK).T.reshape(-1)
    return right_weights(mat[perm])


def pack_weights():
    out = np.zeros((4, SIDE, BLOCK, 8, BLOCK, BLOCK), np.float32)
    for group in range(8):
        for col in range(BLOCK):
            out[group % 4, :, col, group, col, :] = 1.0
    return out.reshape(QUAD, 128).astype(ml_dtypes.bfloat16)


def pack_rows():
    out = np.zeros((2, KMAX, 4, KMAX, 2, BLOCK), np.float32)
    for quad in range(4):
        for slot in range(KMAX):
            out[quad // 2, slot, quad, slot] = 1.0
    return np.tile(out.reshape(8, 128), (1, 3)).astype(ml_dtypes.bfloat16)


def iota(shape, axis):
    return lax.broadcasted_iota(jnp.int32, shape, axis)


def dot(a, b):
    return jnp.dot(a, b, preferred_element_type=F32)


def split(x):
    high = x.astype(BF16)
    return high, (x - high.astype(F32)).astype(BF16)


def times_left(weights, x):
    high, low = split(x)
    return dot(weights, jnp.concatenate([high, low, high, low], axis=0))


def times_right(x, weights_ref):
    high, low = split(x)
    top = weights_ref[0]
    return dot(high, top) + (dot(low, top) + dot(high, weights_ref[1]))


def stack_quads(x):
    return jnp.concatenate([x[:, q * QUAD : (q + 1) * QUAD] for q in range(x.shape[1] // QUAD)], axis=0)


def send_kernel(mom_ref, grad_ref, picks_ref, counts_ref, left_ref, right_ref, pack_ref, fold_ref,
                send_ref, kept_ref, moment_ref):
    step = pl.program_id(0)
    width = mom_ref.shape[1]
    quads = width // QUAD
    moment = 0.9 * mom_ref[...] + grad_ref[...].astype(F32)
    moment_ref[...] = moment
    coef = times_right(stack_quads(times_left(left_ref[...], moment)), right_ref)
    valid = iota(picks_ref.shape, 0) < counts_ref[...]
    picks = jnp.where(valid, picks_ref[...].astype(F32), -1.0)
    groups = picks.shape[1]
    picks8 = jnp.concatenate([picks, jnp.full_like(picks, -1.0)], axis=0)
    spread = iota((groups, width), 0) == step * (width // GROUP) + iota((groups, width), 1) // GROUP
    wide = dot(picks8.astype(BF16), jnp.where(spread, 1.0, 0.0).astype(BF16))
    number = (iota((GROUP, QUAD), 0) // BLOCK) * SIDE + (iota((GROUP, QUAD), 1) % GROUP) // BLOCK
    number = number.astype(F32)
    parts = []
    for q in range(quads):
        quad = coef[q * GROUP : (q + 1) * GROUP]
        total = jnp.zeros_like(quad)
        for k in range(KMAX):
            hit = number == wide[k : k + 1, q * QUAD : (q + 1) * QUAD]
            chosen = jnp.where(hit, quad, 0.0)
            total = total + chosen
            part = chosen[:8]
            for b in range(1, GROUP // 8):
                part = part + chosen[b * 8 : (b + 1) * 8]
            parts.append(part)
        kept_ref[:, q * QUAD : (q + 1) * QUAD] = total
    some = jnp.concatenate(parts, axis=0)
    high, rest = some.astype(BF16), some
    rest = rest - high.astype(F32)
    mid = rest.astype(BF16)
    low = (rest - mid.astype(F32)).astype(BF16)
    lanes = dot(jnp.concatenate([high, mid, low], axis=0), pack_ref[...])
    row = iota((128, 128), 0)
    lane = iota((128, 128), 1)
    fits = ((row % BLOCK) == (lane % BLOCK)) & (((row // 32) % 2) == (lane // 64))
    lanes = jnp.concatenate([jnp.where(fits, lanes[t * 128 : (t + 1) * 128], 0.0) for t in range(3)], axis=0)
    values = dot(fold_ref[...], lanes.astype(BF16))
    for d in range(send_ref.shape[0]):
        send_ref[d, pl.ds(pl.multiple_of(step * 8, 8), 8), :] = values

    @pl.when(step == 0)
    def _():
        padded = jnp.concatenate([picks8, jnp.full((8, 128 - groups), -1.0, F32)], axis=1)
        for d in range(send_ref.shape[0]):
            send_ref[d, ROWS - 8 : ROWS, :] = padded


def momentum_kernel(kept_ref, moment_ref, left_ref, right_ref, out_ref):
    back = times_right(stack_quads(times_left(left_ref[...], kept_ref[...])), right_ref)
    for q in range(back.shape[0] // GROUP):
        cols = slice(q * QUAD, (q + 1) * QUAD)
        out_ref[:, cols] = moment_ref[:, cols] - back[q * GROUP : (q + 1) * GROUP]


def update_kernel(core_ref, own_ref, other_ref, left_ref, right_ref, update_ref, energy_ref,
                  high_ref, low_ref, rows_ref, cols_ref, coef_ref, wide_ref):
    first = core_ref[0] == 0
    half = own_ref.shape[0] // ROWS

    def slab(r):
        a = own_ref[pl.ds(r, half, stride=ROWS), :]
        b = other_ref[pl.ds(r, half, stride=ROWS), :]
        return jnp.concatenate([jnp.where(first, a, b), jnp.where(first, b, a)], axis=0)

    def turned(r):
        return jnp.concatenate([
            jnp.concatenate([slab(r + k), slab(r + k + 1)], axis=0).T for k in range(0, KMAX, 2)
        ], axis=1)

    picks = turned(ROWS - 8)[:GROUP]
    row_block = jnp.floor(picks * (1.0 / SIDE))
    row_high = jnp.floor(row_block * 0.25)
    rows_ref[...] = row_block - 4.0 * row_high
    cols_ref[...] = row_high * SIDE + (picks - SIDE * row_block)
    for t in range(8):
        high, low = split(turned(t * KMAX))
        high_ref[t] = high
        low_ref[t] = low

    slot_of_lane = (iota((8, QUAD), 1) // SIDE) % BLOCK
    slot_of_row = iota((8, QUAD), 0) // BLOCK
    in_low = slot_of_lane == slot_of_row
    in_high = slot_of_lane == slot_of_row + 2
    upper = iota((8, QUAD), 0) < BLOCK
    block_of_row = iota((GROUP, QUAD), 0).astype(F32)

    def eight(t, energy):
        base = pl.multiple_of(t * 8, 8)
        rows8 = rows_ref[pl.ds(base, 8), :]
        cols8 = cols_ref[pl.ds(base, 8), :]
        for g in range(8):
            vals = [high_ref[t, g * 16 : (g + 1) * 16, :].astype(F32),
                    low_ref[t, g * 16 : (g + 1) * 16, :].astype(F32)]
            row = rows8[g : g + 1]
            left = jnp.concatenate([
                jnp.where(row == float(b), v, 0.0).astype(BF16) for b in range(4) for v in vals
            ], axis=0)
            onehot = jnp.where(block_of_row == cols8[g : g + 1], 1.0, 0.0).astype(BF16)
            right = jnp.concatenate([onehot[b * 16 : (b + 1) * 16] for b in range(4) for _ in range(BLOCK)], axis=0)
            out = lax.dot_general(left, right, (((1,), (1,)), ((), ())), preferred_element_type=F32)
            folded = []
            for b in range(4):
                both = out[b * 32 : b * 32 + 16] + out[b * 32 + 16 : b * 32 + 32]
                lanes = jnp.where(in_low, both[:8], jnp.where(in_high, both[8:], 0.0))
                folded.append(lanes + pltpu.roll(lanes, 4, 0))
            for b in range(0, 4, 2):
                coef = jnp.where(upper, folded[b], folded[b + 1])
                coef_ref[pl.ds(pl.multiple_of(t * 128 + g * 16 + b * 4, 8), 8), :] = coef
                energy = energy + coef * coef
        return energy

    energy = lax.fori_loop(0, 8, eight, jnp.zeros((8, QUAD), F32))
    energy_ref[...] = jnp.broadcast_to((energy[:, :128] + energy[:, 128:])[None], energy_ref.shape)
    half_lane = iota((16, 128), 1) < GROUP
    for t in range(4):
        back = times_right(coef_ref[t * QUAD : (t + 1) * QUAD, :], right_ref)
        for pair in range(8):
            even = back[pair * 32 : pair * 32 + 16]
            odd = back[pair * 32 + 16 : pair * 32 + 32]
            lanes = slice((t * 8 + pair) * 128, (t * 8 + pair + 1) * 128)
            for w in range(2):
                e = even[:, w * 128 : (w + 1) * 128]
                o = odd[:, w * 128 : (w + 1) * 128]
                wide_ref[w * 32 : w * 32 + 16, lanes] = jnp.where(half_lane, e, pltpu.roll(o, GROUP, 1))
                wide_ref[w * 32 + 16 : w * 32 + 32, lanes] = jnp.where(half_lane, pltpu.roll(e, GROUP, 1), o)
    for t in range(4):
        lanes = slice(t * 1024, (t + 1) * 1024)
        update_ref[:, lanes] = times_left(left_ref[...], wide_ref[:, lanes])


def weights_kernel(replicas, total_rows, energy_ref, update_ref, weights_ref, out_ref):
    energy = jnp.sum(energy_ref[0])
    for r in range(1, energy_ref.shape[0]):
        energy = energy + jnp.sum(energy_ref[r])
    mean = jnp.broadcast_to(energy * (1.0 / (replicas * replicas * total_rows)), (8, 128))
    factor = (0.5 / replicas) / jnp.sqrt(mean + 1e-06)
    out_ref[...] = weights_ref[...] - update_ref[...] * factor[:1, :1]


def whole(shape):
    return pl.BlockSpec(shape, lambda *_: (0,) * len(shape))


def on_device(momentum, grad, weights, picks, counts):
    width = weights.shape[1]
    nchunk = width // GROUP
    replicas = lax.axis_size("dp")
    nmp = lax.axis_size("mp")
    along_y, along_x, cores = 8, 4, 2
    mat = basis()
    step_width = 1024
    steps = width // step_width
    tile = pl.BlockSpec((GROUP, step_width), lambda s: (0, s))
    left_fwd = jnp.asarray(left_weights(mat))
    left_inv = jnp.asarray(left_weights(mat.T))
    right_fwd = jnp.asarray(right_weights(mat.T))
    right_inv = jnp.asarray(right_weights(mat))
    send, kept, moment = pl.pallas_call(
        send_kernel,
        grid=(steps,),
        in_specs=[tile, tile, whole((KMAX, nchunk)), whole((1, nchunk)), whole((GROUP, QUAD)),
                  whole((2, QUAD, QUAD)), whole((QUAD, 128)), whole((8, 384))],
        out_specs=[whole((along_y, ROWS, 128)), tile, tile],
        out_shape=[jax.ShapeDtypeStruct((along_y, ROWS, 128), F32),
                   jax.ShapeDtypeStruct((GROUP, width), F32),
                   jax.ShapeDtypeStruct((GROUP, width), F32)],
        compiler_params=PARAMS,
        name="send",
    )(momentum[0], grad[0], picks[0, 0].T, counts[0], left_fwd, right_fwd,
      jnp.asarray(pack_weights()), jnp.asarray(pack_rows()))

    def device(y, x, core):
        return (y * along_x + x) * cores + core

    rings_y = [[device(y, x, c) for y in range(along_y)] for x in range(along_x) for c in range(cores)]
    rings_x = [[device(y, x, c) for x in range(along_x)] for y in range(along_y) for c in range(cores)]
    got_y = lax.all_to_all(send, "dp", 0, 0, tiled=True, axis_index_groups=rings_y)
    again = jnp.broadcast_to(got_y.reshape(1, along_y * ROWS, 128), (along_x, along_y * ROWS, 128))
    got_x = lax.all_to_all(again, "dp", 0, 0, tiled=True, axis_index_groups=rings_x)
    own = got_x.reshape(along_x * along_y * ROWS, 128)

    new_momentum = pl.pallas_call(
        momentum_kernel,
        grid=(steps,),
        in_specs=[tile, tile, whole((GROUP, QUAD)), whole((2, QUAD, QUAD))],
        out_specs=tile,
        out_shape=jax.ShapeDtypeStruct((GROUP, width), F32),
        compiler_params=PARAMS,
        cost_estimate=pl.CostEstimate(flops=6 * 2 * 2 * GROUP * GROUP * width, bytes_accessed=12 * GROUP * width,
                                      transcendentals=0),
        name="momentum",
    )(kept, moment, left_inv, right_inv)

    other = lax.ppermute(own, "dp", [(p, p ^ 1) for p in range(replicas)])
    core = (lax.axis_index("dp") % cores).astype(jnp.int32).reshape(1)
    update, energy = pl.pallas_call(
        update_kernel,
        in_specs=[pl.BlockSpec(memory_space=pltpu.SMEM)] + [pl.BlockSpec(memory_space=pltpu.VMEM)] * 4,
        out_shape=[jax.ShapeDtypeStruct((GROUP, width), F32), jax.ShapeDtypeStruct((nmp, 8, 128), F32)],
        scratch_shapes=[
            pltpu.VMEM((8, 128, QUAD), BF16),
            pltpu.VMEM((8, 128, QUAD), BF16),
            pltpu.VMEM((nchunk, QUAD), F32),
            pltpu.VMEM((nchunk, QUAD), F32),
            pltpu.VMEM((nchunk * 16, QUAD), F32),
            pltpu.VMEM((GROUP, width), F32),
        ],
        compiler_params=PARAMS,
        name="update",
    )(core, own, other, left_inv, jnp.asarray(scatter_weights(mat)))
    energies = lax.all_to_all(energy, "mp", 0, 0, tiled=True)
    new_weights = pl.pallas_call(
        functools.partial(weights_kernel, float(replicas), float(GROUP * nmp * width)),
        out_shape=jax.ShapeDtypeStruct((GROUP, width), F32),
        compiler_params=PARAMS,
        name="weights",
    )(energies, update, weights)
    return (new_momentum[None], new_weights)


def solution(mesh):
    in_specs = (
        P("dp", "mp", None),
        P("dp", "mp", None),
        P("mp", None),
        P("dp", "mp", None, None),
        P("dp", "mp", None),
    )
    out_specs = (P("dp", "mp", None), P("mp", None))
    return jax.shard_map(
        on_device, mesh=mesh, in_specs=in_specs, out_specs=out_specs, check_vma=False
    )
```

time: 218 us -> 79.4 us (0.36)
  the two profiles are of different devices: /device:TPU:8 before, /device:TPU:1 now
where the time goes in v1:
time: 79.4 us; the launch traced here: 78.7 us
  blocking collectives  27.2 us (34%)
  starting transfers between devices  21.1 us (27%)
  Pallas kernels  13.7 us (17%)
  local copies, waits for them, and re-layouts  9.65 us (12%)
  waiting for transfers between devices  6.28 us (8%)
    all_to_all x1, blocking collectives, on_device(): lax.all_to_all(send, 'dp', 0, 0, tiled=True, axis_index_groups=rings_y)  15.7 us
    all_to_all x1, starting transfers between devices, on_device(): energies = lax.all_to_all(energy, 'mp', 0, 0, tiled=True)  12.6 us
    all_to_all x1, blocking collectives, on_device(): lax.all_to_all(again, 'dp', 0, 0, tiled=True, axis_index_groups=rings_x)  11.5 us
    unnamed x32, local copies, waits for them, and re-layouts  9.6 us
    ppermute x1, starting transfers between devices, on_device(): other = lax.ppermute(own, 'dp', [(p, p ^ 1) for p in range(replicas)])  8.5 us
    pallas_call x1, Pallas kernels, on_device(): pl.pallas_call(update_kernel, in_specs=[pl.BlockSpec(memory_space=pltpu.S...  5.85 us
    all_to_all x1, waiting for transfers between devices, on_device(): energies = lax.all_to_all(energy, 'mp', 0, 0, tiled=True)  4.59 us
    pallas_call x1, Pallas kernels, on_device(): pl.pallas_call(send_kernel, grid=(steps,), in_specs=[tile, tile, whole((K...  3.66 us
  transfers between devices with their start and end apart: 2, of which 2 were waited for; matrix products, arithmetic and copies ran while one was open for 0% of the time, Pallas kernels for 4%

profile of v1, /device:TPU:1, one launch (start us, length us, event | category | flops | bytes accessed | tf_op | source)
XLA Modules:
  0.0 78.7 jit_solution(8984357327270156558)
XLA Ops:
  0.6 0.0 copy-start.13
  0.6 0.0 copy-start.14
  0.7 0.0 copy-start.15
  0.7 0.7 copy-done.13
  1.3 0.0 copy-done.14
  1.3 0.0 copy-done.15
  1.3 0.0 copy-start.1
  1.3 1.2 %copy-done.1 = f32[1,64,4096]{2,1,0:T(8,128)S(1)} copy-done((f32[1,64,4096]{2,1,0:T(8,128)S(1)}, f32[1,64,4096]{2,1,0:T(8,128)}, u32[]{:S(2)}) %copy-start.1) | copy-done | bytes 1048600
  2.6 0.0 copy-start.6
  2.6 1.0 %copy-done.6 = bf16[1,64,4096]{2,1,0:T(8,128)(2,1)S(1)} copy-done((bf16[1,64,4096]{2,1,0:T(8,128)(2,1)S(1)}, bf16[1,64,4096]{2,1,0:T(8,128)(2,1)}, u32[]{:S(2)}) %copy-start.6) | copy-done | bytes 524312
  3.6 0.0 copy-start.7
  3.6 0.9 %copy-done.7 = bf16[2,256,256]{2,1,0:T(8,128)(2,1)S(1)} copy-done((bf16[2,256,256]{2,1,0:T(8,128)(2,1)S(1)}, bf16[2,256,256]{2,1,0:T(8,128)(2,1)}, u32[]{:S(2)}) %copy-start.7) | copy-done | bytes 262168
  4.6 0.0 copy-start.11
  4.6 0.8 %copy-done.11 = bf16[256,128]{1,0:T(8,128)(2,1)S(1)} copy-done((bf16[256,128]{1,0:T(8,128)(2,1)S(1)}, bf16[256,128]{1,0:T(8,128)(2,1)}, u32[]{:S(2)}) %copy-start.11) | copy-done | bytes 65560
  5.4 0.0 copy-start.12
  5.4 0.8 copy-done.12
  6.2 3.7 %send.1 = (f32[8,40,128]{2,1,0:T(8,128)S(1)}, f32[64,4096]{1,0:T(8,128)S(1)}, f32[64,4096]{1,0:T(8,128)S(1)}) custom-call(f32[64,4096]{1,0:T(8,128)S(1)} %bitcast.12, bf16[64,4096]{1,0:T(8,128)(2,1)S(1)} %bitcast.13, s32[4,64]{1,0:T(4,128)S(1)} %bitcast.14, s32[1,64]{1,0:T(1,128)S(1)} %bitcast.15, bf16[64,256]{1,0:T(8,128)(2,1)S(1)} %copy-done.12, ...), custom_call_target="tpu_custom_call" | custom-call | tf_op jit(solution)/shard_map/send/pallas_call | solution.py:255
  9.8 0.0 copy-start.2
  9.8 15.7 %all_to_all.15 = f32[8,40,128]{2,1,0:T(8,128)S(1)} all-to-all(f32[8,40,128]{2,1,0:T(8,128)S(1)} %get-tuple-element.9), channel_id=1, replica_groups={{0,96,192,288,384,480,576,672},{12,108,204,300,396,492,588,684},{24,120..., dimensions={0} | all-to-all | bytes 327680 | tf_op jit(solution)/shard_map/all_to_all | solution.py:274
  25.6 0.0 copy-start.8
  25.6 11.5 %all_to_all.16 = f32[4,320,128]{2,1,0:T(8,128)S(1)} all-to-all(f32[4,320,128]{2,1,0:T(8,128)S(1)} %broadcast_in_dim.12), channel_id=1, replica_groups={{0,24,48,72},{12,36,60,84},{96,120,144,168},{108,132,156,180},{192,216,..., dimensions={0} | all-to-all | bytes 1310720 | tf_op jit(solution)/shard_map/all_to_all | solution.py:276
  37.1 0.0 copy-done.2
  37.1 0.0 copy-start.10
  37.1 8.5 %collective-permute-start = (f32[1280,128]{1,0:T(8,128)S(1)}, f32[1280,128]{1,0:T(8,128)S(1)}, u32[]{:S(2)}, u32[]{:S(2)}) collective-permute-start(f32[1280,128]{1,0:T(8,128)S(1)} %bitcast.10), channel_id=1, source_target_pairs={{0,12},{12,0},{24,36},{36,24},{48,60},{60,48},{72,84},{84,72},{96,... | collective-permute-start | bytes 1966088 | tf_op jit(solution)/shard_map/ppermute | solution.py:291
  45.6 1.7 %collective-permute-done.other_ref = f32[1280,128]{1,0:T(8,128)S(1)} collective-permute-done((f32[1280,128]{1,0:T(8,128)S(1)}, f32[1280,128]{1,0:T(8,128)S(1)}, u32[]{:S(2)}, u32[]{:S(2)}) %collective-permute-start) | collective-permute-done | bytes 655392 | tf_op jit(solution)/shard_map/ppermute | solution.py:291
  47.3 0.0 copy-start.4
  47.3 0.8 %copy-done.4 = f32[1280,128]{1,0:T(8,128)} copy-done((f32[1280,128]{1,0:T(8,128)}, f32[1280,128]{1,0:T(8,128)S(1)}, u32[]{:S(2)}) %copy-start.4) | copy-done | bytes 655384
  48.1 0.0 copy-done.8
  48.1 0.0 copy-done.10
  48.1 0.0 copy-start.5
  48.1 1.1 %copy-done.5 = f32[1280,128]{1,0:T(8,128)S(1)} copy-done((f32[1280,128]{1,0:T(8,128)S(1)}, f32[1280,128]{1,0:T(8,128)}, u32[]{:S(2)}) %copy-start.5) | copy-done | bytes 655384
  49.2 5.9 %update.1 = (f32[64,4096]{1,0:T(8,128)S(1)}, f32[12,8,128]{2,1,0:T(8,128)}) custom-call(s32[1]{0:T(128)} %bitcast.6.core_ref, f32[1280,128]{1,0:T(8,128)S(1)} %bitcast.11, f32[1280,128]{1,0:T(8,128)S(1)} %copy-done.5, bf16[64,256]{1,0:T(8,128)(2,1)S(1)} %copy-done.10, bf16[2,256,256]{2,1,0:T(8,128)(2,1)S(1)} %copy-done.8), custom_call_target="tpu_custom_call" | custom-call | tf_op jit(solution)/shard_map/update/pallas_call | solution.py:293
  55.1 12.6 %all-to-all-start.2 = ((f32[12,8,128]{2,1,0:T(8,128)}), f32[12,8,128]{2,1,0:T(8,128)S(1)}, u32[]{:S(2)}, u32[]{:S(2)}) async-start(f32[12,8,128]{2,1,0:T(8,128)} %get-tuple-element.10), calls=%async_computation.2 | async-start | bytes 98304 | tf_op jit(solution)/shard_map/all_to_all | solution.py:308
  67.7 0.0 copy-start.3
  67.7 1.2 %copy-done.3 = f32[64,4096]{1,0:T(8,128)S(1)} copy-done((f32[64,4096]{1,0:T(8,128)S(1)}, f32[64,4096]{1,0:T(8,128)}, u32[]{:S(2)}) %copy-start.3) | copy-done | bytes 1048600
  68.9 0.0 copy-start.9
  68.9 0.9 %copy-done.9 = bf16[2,256,256]{2,1,0:T(8,128)(2,1)S(1)} copy-done((bf16[2,256,256]{2,1,0:T(8,128)(2,1)S(1)}, bf16[2,256,256]{2,1,0:T(8,128)(2,1)}, u32[]{:S(2)}) %copy-start.9) | copy-done | bytes 262168
  69.9 0.0 copy-start
  69.9 2.9 %momentum.1 = f32[64,4096]{1,0:T(8,128)} custom-call(f32[64,4096]{1,0:T(8,128)S(1)} %get-tuple-element.7.kept_ref, f32[64,4096]{1,0:T(8,128)S(1)} %copy-done.3, bf16[64,256]{1,0:T(8,128)(2,1)S(1)} %copy-done.10, bf16[2,256,256]{2,1,0:T(8,128)(2,1)S(1)} %copy-done.9), custom_call_target="tpu_custom_call" | custom-call | flops 402653184 | bytes 3145728 | tf_op jit(solution)/shard_map/momentum/pallas_call | solution.py:279
  72.8 4.6 %all-to-all-done.2.energy_ref = f32[12,8,128]{2,1,0:T(8,128)S(1)} async-done(((f32[12,8,128]{2,1,0:T(8,128)}), f32[12,8,128]{2,1,0:T(8,128)S(1)}, u32[]{:S(2)}, u32[]{:S(2)}) %all-to-all-start.2) | async-done | bytes 49184 | tf_op jit(solution)/shard_map/all_to_all | solution.py:308
  77.4 0.0 copy-done
  77.4 1.3 %weights.1 = f32[64,4096]{1,0:T(8,128)} custom-call(f32[12,8,128]{2,1,0:T(8,128)S(1)} %all-to-all-done.2.energy_ref, f32[64,4096]{1,0:T(8,128)S(1)} %get-tuple-element.11.update_ref, f32[64,4096]{1,0:T(8,128)S(1)} %copy-done), custom_call_target="tpu_custom_call" | custom-call | tf_op jit(solution)/shard_map/weights/pallas_call | solution.py:309
  (1 shorter events, 0.0 us)
Async XLA Ops:
  0.6 0.7 copy-start.13
  0.6 0.7 copy-start.14
  0.7 0.7 copy-start.15
  1.3 1.2 %copy-start.1 = (f32[1,64,4096]{2,1,0:T(8,128)S(1)}, f32[1,64,4096]{2,1,0:T(8,128)}, u32[]{:S(2)}) copy-start(f32[1,64,4096]{2,1,0:T(8,128)} %param.12) | copy-start | bytes 3145732
  2.6 1.0 %copy-start.6 = (bf16[1,64,4096]{2,1,0:T(8,128)(2,1)S(1)}, bf16[1,64,4096]{2,1,0:T(8,128)(2,1)}, u32[]{:S(2)}) copy-start(bf16[1,64,4096]{2,1,0:T(8,128)(2,1)} %param.13) | copy-start | bytes 1572868
  3.6 0.9 %copy-start.7 = (bf16[2,256,256]{2,1,0:T(8,128)(2,1)S(1)}, bf16[2,256,256]{2,1,0:T(8,128)(2,1)}, u32[]{:S(2)}) copy-start(bf16[2,256,256]{2,1,0:T(8,128)(2,1)} %constant.34.clone.right_ref) | copy-start | bytes 786436
  4.6 0.8 %copy-start.11 = (bf16[256,128]{1,0:T(8,128)(2,1)S(1)}, bf16[256,128]{1,0:T(8,128)(2,1)}, u32[]{:S(2)}) copy-start(bf16[256,128]{1,0:T(8,128)(2,1)} %constant.36.clone.pack_ref) | copy-start | bytes 196612
  5.4 0.8 copy-start.12
  9.8 27.3 %copy-start.2 = (f32[64,4096]{1,0:T(8,128)}, f32[64,4096]{1,0:T(8,128)S(1)}, u32[]{:S(2)}) copy-start(f32[64,4096]{1,0:T(8,128)S(1)} %get-tuple-element.8.moment_ref) | copy-start | bytes 3145732
  25.6 22.5 %copy-start.8 = (bf16[2,256,256]{2,1,0:T(8,128)(2,1)S(1)}, bf16[2,256,256]{2,1,0:T(8,128)(2,1)}, u32[]{:S(2)}) copy-start(bf16[2,256,256]{2,1,0:T(8,128)(2,1)} %constant.38.clone.right_ref) | copy-start | bytes 786436
  37.1 11.1 %copy-start.10 = (bf16[64,256]{1,0:T(8,128)(2,1)S(1)}, bf16[64,256]{1,0:T(8,128)(2,1)}, u32[]{:S(2)}) copy-start(bf16[64,256]{1,0:T(8,128)(2,1)} %constant.33.clone.left_ref) | copy-start | bytes 98308
  37.1 10.2 %collective-permute-start = (f32[1280,128]{1,0:T(8,128)S(1)}, f32[1280,128]{1,0:T(8,128)S(1)}, u32[]{:S(2)}, u32[]{:S(2)}) collective-permute-start(f32[1280,128]{1,0:T(8,128)S(1)} %bitcast.10), channel_id=1, source_target_pairs={{0,12},{12,0},{24,36},{36,24},{48,60},{60,48},{72,84},{84,72},{96,... | collective-permute-start | bytes 1966088 | tf_op jit(solution)/shard_map/ppermute | solution.py:291
  47.3 0.8 %copy-start.4 = (f32[1280,128]{1,0:T(8,128)}, f32[1280,128]{1,0:T(8,128)S(1)}, u32[]{:S(2)}) copy-start(f32[1280,128]{1,0:T(8,128)S(1)} %collective-permute-done.other_ref) | copy-start | bytes 1966084
  48.1 1.1 %copy-start.5 = (f32[1280,128]{1,0:T(8,128)S(1)}, f32[1280,128]{1,0:T(8,128)}, u32[]{:S(2)}) copy-start(f32[1280,128]{1,0:T(8,128)} %copy-done.4) | copy-start | bytes 1966084
  55.1 22.3 %all-to-all-start.2 = ((f32[12,8,128]{2,1,0:T(8,128)}), f32[12,8,128]{2,1,0:T(8,128)S(1)}, u32[]{:S(2)}, u32[]{:S(2)}) async-start(f32[12,8,128]{2,1,0:T(8,128)} %get-tuple-element.10), calls=%async_computation.2 | async-start | bytes 98304 | tf_op jit(solution)/shard_map/all_to_all | solution.py:308
  67.7 1.2 %copy-start.3 = (f32[64,4096]{1,0:T(8,128)S(1)}, f32[64,4096]{1,0:T(8,128)}, u32[]{:S(2)}) copy-start(f32[64,4096]{1,0:T(8,128)} %copy-done.2) | copy-start | bytes 3145732
  68.9 0.9 %copy-start.9 = (bf16[2,256,256]{2,1,0:T(8,128)(2,1)S(1)}, bf16[2,256,256]{2,1,0:T(8,128)(2,1)}, u32[]{:S(2)}) copy-start(bf16[2,256,256]{2,1,0:T(8,128)(2,1)} %constant.35.clone.right_ref) | copy-start | bytes 786436
  69.9 7.5 %copy-start = (f32[64,4096]{1,0:T(8,128)S(1)}, f32[64,4096]{1,0:T(8,128)}, u32[]{:S(2)}) copy-start(f32[64,4096]{1,0:T(8,128)} %weights_ref.1) | copy-start | bytes 3145732

commit v2 on v1

v2 whole, which is shorter than its diff:
```python
import functools

import jax
import jax.numpy as jnp
import ml_dtypes
import numpy as np
from jax import lax
from jax.experimental import pallas as pl
from jax.experimental.pallas import tpu as pltpu
from jax.sharding import PartitionSpec as P

GROUP = 64
BLOCK = 4
KMAX = 4
SIDE = GROUP // BLOCK
QUAD = 4 * GROUP
ROWS = 17
F32 = jnp.float32
BF16 = jnp.bfloat16
PARAMS = pltpu.CompilerParams(vmem_limit_bytes=24 * 1024 * 1024)


def basis():
    rows = np.arange(GROUP, dtype=np.float64)[:, None]
    cols = np.arange(GROUP, dtype=np.float64)[None, :]
    waves = np.cos(np.pi * (2.0 * cols + 1.0) * rows / (2.0 * GROUP))
    factor = np.where(rows == 0.0, np.sqrt(1.0 / GROUP), np.sqrt(2.0 / GROUP))
    return (waves * factor).astype(np.float32)


def halves(mat):
    high = mat.astype(ml_dtypes.bfloat16)
    low = (mat - high.astype(np.float32)).astype(ml_dtypes.bfloat16)
    return high, low


def left_weights(mat):
    high, low = halves(mat)
    return np.concatenate([high, high, low, low], axis=1)


def right_weights(mat):
    return np.stack(halves(np.kron(np.eye(4, dtype=np.float32), mat)))


def scatter_weights(mat):
    perm = np.arange(GROUP).reshape(SIDE, BLOCK).T.reshape(-1)
    return right_weights(mat[perm])


def iota(shape, axis):
    return lax.broadcasted_iota(jnp.int32, shape, axis)


def dot(a, b):
    return jnp.dot(a, b, preferred_element_type=F32)


def split(x):
    high = x.astype(BF16)
    return high, (x - high.astype(F32)).astype(BF16)


def times_left(weights, x):
    high, low = split(x)
    return dot(weights, jnp.concatenate([high, low, high, low], axis=0))


def stack_quads(x):
    return jnp.concatenate([x[:, q * QUAD : (q + 1) * QUAD] for q in range(x.shape[1] // QUAD)], axis=0)


def transform_weights(left, right):
    return np.concatenate([left, right[0], right[1]], axis=0)


def times_right(x, weights):
    high, low = split(x)
    top = weights[GROUP : GROUP + QUAD]
    return dot(high, top) + (dot(low, top) + dot(high, weights[GROUP + QUAD :]))


def flag(cond):
    return jnp.where(cond, 1.0, 0.0).astype(BF16)


def numbers():
    number = (iota((GROUP, QUAD), 0) // BLOCK) * SIDE + (iota((GROUP, QUAD), 1) % GROUP) // BLOCK
    return number.astype(F32)


def listed(picks, counts):
    valid = iota(picks.shape, 0) < counts
    return jnp.where(valid, picks.astype(F32), -1.0)


def spread_lanes(picks, width, start):
    groups = picks.shape[1]
    eight = jnp.concatenate([picks, jnp.full_like(picks, -1.0)], axis=0).astype(BF16)
    member = flag(iota((groups, width), 0) == start + iota((groups, width), 1) // GROUP)
    return dot(eight, member)


def send_kernel(mom_hbm, grad_hbm, picks_hbm, counts_hbm, weights_hbm, send_ref,
                mom_ref, grad_ref, picks_ref, counts_ref, weights_ref, sems):
    copies = [
        pltpu.make_async_copy(src, dst, sems.at[i])
        for i, (src, dst) in enumerate((
            (picks_hbm, picks_ref), (counts_hbm, counts_ref), (weights_hbm, weights_ref),
            (mom_hbm, mom_ref), (grad_hbm, grad_ref)))
    ]
    for copy in copies:
        copy.start()
    width = mom_ref.shape[1]
    quads = width // QUAD

    row = iota((QUAD, 128), 0)
    lane = iota((QUAD, 128), 1)
    pack = flag((row // GROUP == (lane // 16) % 4) & (row % BLOCK == (lane // BLOCK) % BLOCK))
    row = iota((8, 384), 0)
    lane = iota((8, 384), 1)
    fold = flag((row // KMAX == (lane % 128) // 64) & (row % KMAX == (lane // 8) % KMAX))
    row = iota((128, 128), 0)
    lane = iota((128, 128), 1)
    fits = ((row % BLOCK) == (lane % BLOCK)) & (((row // 32) % 2) == (lane // 64))
    number = numbers()

    for copy in copies[:3]:
        copy.wait()
    picks = listed(picks_ref[...], counts_ref[...])
    groups = picks.shape[1]
    wide = spread_lanes(picks, width, 0)
    weights = weights_ref[...]
    for copy in copies[3:]:
        copy.wait()
    moment = 0.9 * mom_ref[...] + grad_ref[...].astype(F32)
    coef = times_right(stack_quads(times_left(weights[:GROUP], moment)), weights)
    packed = []
    for first in range(0, quads, 4):
        parts = []
        for q in range(first, first + 4):
            quad = coef[q * GROUP : (q + 1) * GROUP]
            for k in range(KMAX):
                chosen = jnp.where(number == wide[k : k + 1, q * QUAD : (q + 1) * QUAD], quad, 0.0)
                some = chosen[:8]
                for b in range(1, GROUP // 8):
                    some = some + chosen[b * 8 : (b + 1) * 8]
                parts.append(some)
        some = jnp.concatenate(parts, axis=0)
        high = some.astype(BF16)
        rest = some - high.astype(F32)
        mid = rest.astype(BF16)
        low = (rest - mid.astype(F32)).astype(BF16)
        lanes = dot(jnp.concatenate([high, mid, low], axis=0), pack)
        lanes = jnp.concatenate([jnp.where(fits, lanes[t * 128 : (t + 1) * 128], 0.0) for t in range(3)], axis=0)
        packed.append(dot(fold, lanes.astype(BF16)))
    part = groups // 2
    both = []
    for h in range(2):
        row = jnp.concatenate([picks[k : k + 1, h * part : (h + 1) * part] for k in range(KMAX)], axis=1)
        both += [packed[2 * h], packed[2 * h + 1], row]
    again = jnp.concatenate(both * 4, axis=0)
    for d in range(send_ref.shape[0] // again.shape[0]):
        send_ref[d * again.shape[0] : (d + 1) * again.shape[0], :] = again


def momentum_kernel(mom_ref, grad_ref, picks_ref, counts_ref, forward_ref, inverse_ref, out_ref):
    width = mom_ref.shape[1]
    picks = listed(picks_ref[...], counts_ref[...])
    wide = spread_lanes(picks, width, pl.program_id(0) * (width // GROUP))
    forward = forward_ref[...]
    inverse = inverse_ref[...]
    number = numbers()
    moment = 0.9 * mom_ref[...] + grad_ref[...].astype(F32)
    coef = times_right(stack_quads(times_left(forward[:GROUP], moment)), forward)
    kept = []
    for q in range(width // QUAD):
        lanes = wide[:, q * QUAD : (q + 1) * QUAD]
        hit = number == lanes[:1]
        for k in range(1, KMAX):
            hit = hit | (number == lanes[k : k + 1])
        kept.append(jnp.where(hit, coef[q * GROUP : (q + 1) * GROUP], 0.0))
    back = times_right(stack_quads(times_left(inverse[:GROUP], jnp.concatenate(kept, axis=1))), inverse)
    for q in range(width // QUAD):
        cols = slice(q * QUAD, (q + 1) * QUAD)
        out_ref[:, cols] = moment[:, cols] - back[q * GROUP : (q + 1) * GROUP]


def scatter_kernel(got_ref, _, coef_ref, energy_ref, high_ref, low_ref, rows_ref, cols_ref):
    replicas = got_ref.shape[0] // ROWS
    eights = (ROWS - 1) // KMAX
    groups = eights * 8

    def slab(r):
        return got_ref[pl.ds(r, replicas, stride=ROWS), :]

    picks = slab(ROWS - 1)
    picks = jnp.concatenate([picks, picks], axis=0).T
    first = iota((groups, 128), 1) < replicas
    picks = jnp.concatenate([
        jnp.where(first, picks[k * groups : (k + 1) * groups], picks[(k + 1) * groups : (k + 2) * groups])
        for k in range(0, KMAX, 2)
    ], axis=1)
    row_block = jnp.floor(picks * (1.0 / SIDE))
    row_high = jnp.floor(row_block * 0.25)
    rows_ref[...] = row_block - 4.0 * row_high
    cols_ref[...] = row_high * SIDE + (picks - SIDE * row_block)
    for t in range(eights):
        turned = jnp.concatenate([
            jnp.concatenate([slab(t * KMAX + k), slab(t * KMAX + k + 1)], axis=0).T for k in range(0, KMAX, 2)
        ], axis=1)
        high, low = split(turned)
        high_ref[t] = high
        low_ref[t] = low

    slot_of_lane = (iota((8, QUAD), 1) // SIDE) % BLOCK
    slot_of_row = iota((8, QUAD), 0) // BLOCK
    in_low = slot_of_lane == slot_of_row
    in_high = slot_of_lane == slot_of_row + 2
    upper = iota((8, QUAD), 0) < BLOCK
    block_of_row = iota((GROUP, QUAD), 0).astype(F32)

    def eight(t, energy):
        base = pl.multiple_of(t * 8, 8)
        rows8 = rows_ref[pl.ds(base, 8), :]
        cols8 = cols_ref[pl.ds(base, 8), :]
        for g in range(8):
            vals = [high_ref[t, g * 16 : (g + 1) * 16, :].astype(F32),
                    low_ref[t, g * 16 : (g + 1) * 16, :].astype(F32)]
            row = rows8[g : g + 1]
            left = jnp.concatenate([
                jnp.where(row == float(b), v, 0.0).astype(BF16) for b in range(4) for v in vals
            ], axis=0)
            onehot = flag(block_of_row == cols8[g : g + 1])
            right = jnp.concatenate([onehot[b * 16 : (b + 1) * 16] for b in range(4) for _ in range(BLOCK)], axis=0)
            out = lax.dot_general(left, right, (((1,), (1,)), ((), ())), preferred_element_type=F32)
            folded = []
            for b in range(4):
                both = out[b * 32 : b * 32 + 16] + out[b * 32 + 16 : b * 32 + 32]
                lanes = jnp.where(in_low, both[:8], jnp.where(in_high, both[8:], 0.0))
                folded.append(lanes + pltpu.roll(lanes, 4, 0))
            for b in range(0, 4, 2):
                coef = jnp.where(upper, folded[b], folded[b + 1])
                coef_ref[pl.ds(pl.multiple_of(t * 128 + g * 16 + b * 4, 8), 8), :] = coef
                energy = energy + coef * coef
        return energy

    energy = lax.fori_loop(0, eights, eight, jnp.zeros((8, QUAD), F32))
    energy = jnp.sum(energy[:, :128] + energy[:, 128:], axis=0, keepdims=True)
    energy_ref[...] = jnp.broadcast_to(energy, energy_ref.shape)


def inverse_kernel(coef_ref, weights_ref, update_ref, wide_ref):
    weights = weights_ref[...]
    half_lane = iota((16, 128), 1) < GROUP
    for t in range(coef_ref.shape[0] // QUAD):
        back = times_right(coef_ref[t * QUAD : (t + 1) * QUAD, :], weights)
        for pair in range(8):
            even = back[pair * 32 : pair * 32 + 16]
            odd = back[pair * 32 + 16 : pair * 32 + 32]
            lanes = slice((t * 8 + pair) * 128, (t * 8 + pair + 1) * 128)
            for w in range(2):
                e = even[:, w * 128 : (w + 1) * 128]
                o = odd[:, w * 128 : (w + 1) * 128]
                wide_ref[w * 32 : w * 32 + 16, lanes] = jnp.where(half_lane, e, pltpu.roll(o, GROUP, 1))
                wide_ref[w * 32 + 16 : w * 32 + 32, lanes] = jnp.where(half_lane, pltpu.roll(e, GROUP, 1), o)
        lanes = slice(t * 1024, (t + 1) * 1024)
        update_ref[:, lanes] = times_left(weights[:GROUP], wide_ref[:, lanes])


def weights_kernel(replicas, total_rows, core_ref, energy_ref, own_ref, other_ref, weights_ref, out_ref):
    mean = jnp.broadcast_to(jnp.sum(energy_ref[...]) * (1.0 / (replicas * replicas * total_rows)), (8, 128))
    factor = ((0.5 / replicas) / jnp.sqrt(mean + 1e-06))[:1, :1]
    half = own_ref.shape[1]
    mine = core_ref[0] * half
    for mult, ref in ((mine, own_ref), (half - mine, other_ref)):
        cols = pl.ds(pl.multiple_of(mult, half), half)
        out_ref[:, cols] = weights_ref[:, cols] - ref[...] * factor


def whole(shape):
    return pl.BlockSpec(shape, lambda *_: (0,) * len(shape))


def on_device(momentum, grad, weights, picks, counts):
    width = weights.shape[1]
    nchunk = width // GROUP
    replicas = lax.axis_size("dp")
    nmp = lax.axis_size("mp")
    mat = basis()
    step_width = 1024
    steps = width // step_width
    half = width // 2
    tile = pl.BlockSpec((GROUP, step_width), lambda s: (0, s))
    forward = jnp.asarray(transform_weights(left_weights(mat), right_weights(mat.T)))
    inverse = jnp.asarray(transform_weights(left_weights(mat.T), right_weights(mat)))
    scatter = jnp.asarray(transform_weights(left_weights(mat.T), scatter_weights(mat)))
    hbm = pl.BlockSpec(memory_space=pltpu.HBM)
    vmem = pl.BlockSpec(memory_space=pltpu.VMEM)
    taken = [pltpu.with_memory_space_constraint(x, pltpu.HBM)
             for x in (momentum[0], grad[0], picks[0, 0].T, counts[0], forward)]
    send = pl.pallas_call(
        send_kernel,
        in_specs=[hbm] * 5,
        out_shape=jax.ShapeDtypeStruct((replicas * ROWS, 128), F32),
        scratch_shapes=[
            pltpu.VMEM((GROUP, width), F32),
            pltpu.VMEM((GROUP, width), BF16),
            pltpu.VMEM((KMAX, nchunk), jnp.int32),
            pltpu.VMEM((1, nchunk), jnp.int32),
            pltpu.VMEM(forward.shape, BF16),
            pltpu.SemaphoreType.DMA((5,)),
        ],
        compiler_params=PARAMS,
        name="send",
    )(*taken)

    got = lax.all_to_all(send.reshape(replicas * ROWS, 1, 128), "dp", 0, 0, tiled=True)
    new_momentum = pl.pallas_call(
        momentum_kernel,
        grid=(steps,),
        in_specs=[tile, tile, whole((KMAX, nchunk)), whole((1, nchunk)), whole(forward.shape), whole(inverse.shape)],
        out_specs=tile,
        out_shape=jax.ShapeDtypeStruct((GROUP, width), F32),
        compiler_params=PARAMS,
        cost_estimate=pl.CostEstimate(flops=12 * 2 * 2 * GROUP * GROUP * width, bytes_accessed=10 * GROUP * width,
                                      transcendentals=0),
        name="momentum",
    )(*taken, pltpu.with_memory_space_constraint(inverse, pltpu.HBM))
    coef, energy = pl.pallas_call(
        scatter_kernel,
        in_specs=[vmem, hbm],
        out_shape=[jax.ShapeDtypeStruct((half // 4, QUAD), F32), jax.ShapeDtypeStruct((2 * nmp, 128), F32)],
        scratch_shapes=[
            pltpu.VMEM((nchunk // 16, 128, QUAD), BF16),
            pltpu.VMEM((nchunk // 16, 128, QUAD), BF16),
            pltpu.VMEM((nchunk // 2, QUAD), F32),
            pltpu.VMEM((nchunk // 2, QUAD), F32),
        ],
        compiler_params=PARAMS,
        name="scatter",
    )(got.reshape(replicas * ROWS, 128), pltpu.with_memory_space_constraint(new_momentum, pltpu.HBM))
    partners = [[(2 * chip + core) * nmp + z for core in range(2) for z in range(nmp)] for chip in range(replicas // 2)]
    energies = lax.all_to_all(energy.reshape(2 * nmp, 1, 128), ("dp", "mp"), 0, 0, tiled=True,
                              axis_index_groups=partners).reshape(2 * nmp, 128)
    own = pl.pallas_call(
        inverse_kernel,
        out_shape=jax.ShapeDtypeStruct((GROUP, half), F32),
        scratch_shapes=[pltpu.VMEM((GROUP, half), F32)],
        compiler_params=PARAMS,
        cost_estimate=pl.CostEstimate(flops=6 * 2 * GROUP * GROUP * half, bytes_accessed=8 * GROUP * half,
                                      transcendentals=0),
        name="inverse",
    )(coef, scatter)
    other = lax.ppermute(own, "dp", [(p, p ^ 1) for p in range(replicas)])
    core = jnp.bitwise_and(lax.axis_index("dp"), 1).astype(jnp.int32).reshape(1)
    new_weights = pl.pallas_call(
        functools.partial(weights_kernel, float(replicas), float(GROUP * nmp * width)),
        in_specs=[pl.BlockSpec(memory_space=pltpu.SMEM)] + [vmem] * 4,
        out_shape=jax.ShapeDtypeStruct((GROUP, width), F32),
        compiler_params=PARAMS,
        name="weights",
    )(core, energies, own, other, weights)
    return (new_momentum[None], new_weights)


def solution(mesh):
    in_specs = (
        P("dp", "mp", None),
        P("dp", "mp", None),
        P("mp", None),
        P("dp", "mp", None, None),
        P("dp", "mp", None),
    )
    out_specs = (P("dp", "mp", None), P("mp", None))
    return jax.shard_map(
        on_device, mesh=mesh, in_specs=in_specs, out_specs=out_specs, check_vma=False
    )
```

time: 79.4 us -> 67.9 us (0.86)
  blocking collectives: 27.2 us -> 0 us
  waiting for transfers between devices: 6.28 us -> 21.9 us
  local copies, waits for them, and re-layouts: 9.65 us -> 0.01 us
  starting transfers between devices: 21.1 us -> 29.2 us
  Pallas kernels: 13.7 us -> 15.8 us
    all_to_all x2 -> x0, blocking collectives: 27.2 us -> none  [the longest x1 15.7 us: on_device(): lax.all_to_all(send, 'dp', 0, 0, tiled=True, axis_index_groups=rings_y)]
    all_to_all x1 -> x2, waiting for transfers between devices: 4.59 us -> 21.9 us  [the longest x1 12.6 us: on_device(): lax.all_to_all(send.reshape(replicas * ROWS, 1, 128), 'dp', 0, 0, tiled=T...]
    all_to_all x1 -> x2, starting transfers between devices: 12.6 us -> 26.9 us  [the longest x1 14.6 us: on_device(): lax.all_to_all(send.reshape(replicas * ROWS, 1, 128), 'dp', 0, 0, tiled=T...]
    unnamed x32 -> x4, local copies, waits for them, and re-layouts: 9.6 us -> 0.01 us
    ppermute x1, starting transfers between devices: 8.5 us -> 2.32 us  [on_device(): other = lax.ppermute(own, 'dp', [(p, p ^ 1) for p in range(replicas)])]
    pallas_call x1, Pallas kernels: 2.91 us -> 5.92 us  [on_device(): pl.pallas_call(momentum_kernel, grid=(steps,), in_specs=[tile, tile, whol...]
    ppermute x1, waiting for transfers between devices: 1.69 us -> 0.01 us  [on_device(): other = lax.ppermute(own, 'dp', [(p, p ^ 1) for p in range(replicas)])]
    pallas_call x2 -> x3, Pallas kernels: 9.52 us -> 8.63 us  [the longest x1 4.62 us: on_device(): pl.pallas_call(send_kernel, in_specs=[hbm] * 5, out_shape=jax.ShapeDtypeS...]
  transfers between devices with their start and end apart: 2 -> 3, of which waited for: 2 -> 2; matrix products, arithmetic and copies ran while one was open for 0% -> 0% of each run, Pallas kernels for 4% -> 9%
where the time goes in v2:
time: 67.9 us; the launch traced here: 67.5 us
  starting transfers between devices  29.2 us (43%)
  waiting for transfers between devices  21.9 us (32%)
  Pallas kernels  15.8 us (23%)
  between operations  0.68 us (1%)
    all_to_all x1, starting transfers between devices, on_device(): lax.all_to_all(send.reshape(replicas * ROWS, 1, 128), 'dp', 0, 0, tiled=T...  14.6 us
    all_to_all x1, waiting for transfers between devices, on_device(): lax.all_to_all(send.reshape(replicas * ROWS, 1, 128), 'dp', 0, 0, tiled=T...  12.6 us
    all_to_all x1, starting transfers between devices, on_device(): lax.all_to_all(energy.reshape(2 * nmp, 1, 128), ('dp', 'mp'), 0, 0, tiled...  12.3 us
    all_to_all x1, waiting for transfers between devices, on_device(): lax.all_to_all(energy.reshape(2 * nmp, 1, 128), ('dp', 'mp'), 0, 0, tiled...  9.26 us
    pallas_call x1, Pallas kernels, on_device(): pl.pallas_call(momentum_kernel, grid=(steps,), in_specs=[tile, tile, whol...  5.92 us
    pallas_call x1, Pallas kernels, on_device(): pl.pallas_call(send_kernel, in_specs=[hbm] * 5, out_shape=jax.ShapeDtypeS...  4.62 us
    pallas_call x1, Pallas kernels, on_device(): pl.pallas_call(scatter_kernel, in_specs=[vmem, hbm], out_shape=[jax.Shape...  2.85 us
    ppermute x1, starting transfers between devices, on_device(): other = lax.ppermute(own, 'dp', [(p, p ^ 1) for p in range(replicas)])  2.32 us
  transfers between devices with their start and end apart: 3, of which 2 were waited for; matrix products, arithmetic and copies ran while one was open for 0% of the time, Pallas kernels for 9%

profile of v2, /device:TPU:1, one launch (start us, length us, event | category | flops | bytes accessed | tf_op | source)
XLA Modules:
  0.0 67.5 jit_solution(15943030131591652975)
XLA Ops:
  0.6 4.6 %send.1 = f32[1088,128]{1,0:T(8,128)} custom-call(f32[64,4096]{1,0:T(8,128)} %bitcast.18, bf16[64,4096]{1,0:T(8,128)(2,1)} %bitcast.21, s32[4,64]{1,0:T(4,128)} %bitcast.23, s32[1,64]{1,0:T(1,128)} %bitcast.25, bf16[576,256]{1,0:T(8,128)(2,1)} %constant.13.clone.forward_ref.weights_hbm), custom_call_target="tpu_custom_call" | custom-call | tf_op jit(solution)/shard_map/send/pallas_call | solution.py:302
  5.3 14.6 %all-to-all-start = ((f32[1088,1,128]{2,1,0:T(1,128)}), f32[1088,1,128]{2,1,0:T(1,128)S(1)}, u32[]{:S(2)}, u32[]{:S(2)}) async-start(f32[1088,1,128]{2,1,0:T(1,128)} %bitcast.9), calls=%async_computation | async-start | bytes 1114112 | tf_op jit(solution)/shard_map/all_to_all | solution.py:318
  19.9 5.9 %momentum.1._ = f32[64,4096]{1,0:T(8,128)} custom-call(f32[64,4096]{1,0:T(8,128)} %bitcast.19, bf16[64,4096]{1,0:T(8,128)(2,1)} %bitcast.22, s32[4,64]{1,0:T(4,128)} %bitcast.24, s32[1,64]{1,0:T(1,128)} %bitcast.26, bf16[576,256]{1,0:T(8,128)(2,1)} %constant.13.clone.forward_ref.weights_hbm, bf16[576,256]{1,0:T(8,128)(2,1)} %constant.14.clone.inverse_ref), custom_call_target="tpu_custom_call" | custom-call | flops 805306368 | bytes 2621440 | tf_op jit(solution)/shard_map/momentum/pallas_call | solution.py:319
  25.8 12.6 %all-to-all-done = f32[1088,1,128]{2,1,0:T(1,128)S(1)} async-done(((f32[1088,1,128]{2,1,0:T(1,128)}), f32[1088,1,128]{2,1,0:T(1,128)S(1)}, u32[]{:S(2)}, u32[]{:S(2)}) %all-to-all-start) | async-done | bytes 557088 | tf_op jit(solution)/shard_map/all_to_all | solution.py:318
  38.4 0.0 copy-start.1
  38.4 2.8 %scatter.1 = (f32[512,256]{1,0:T(8,128)S(1)}, f32[24,128]{1,0:T(8,128)}) custom-call(f32[1088,128]{1,0:T(8,128)S(1)} %bitcast.16, f32[64,4096]{1,0:T(8,128)} %momentum.1._), custom_call_target="tpu_custom_call" | custom-call | tf_op jit(solution)/shard_map/scatter/pallas_call | solution.py:330
  41.2 0.0 copy-start
  41.2 0.0 copy-done.1
  41.2 1.2 %inverse.1.own_ref = f32[64,2048]{1,0:T(8,128)S(1)} custom-call(f32[512,256]{1,0:T(8,128)S(1)} %get-tuple-element.5.coef_ref, bf16[576,256]{1,0:T(8,128)(2,1)S(1)} %copy-done.1), custom_call_target="tpu_custom_call" | custom-call | flops 100663296 | bytes 1048576 | tf_op jit(solution)/shard_map/inverse/pallas_call | solution.py:346
  42.4 2.3 %collective-permute-start = (f32[64,2048]{1,0:T(8,128)S(1)}, f32[64,2048]{1,0:T(8,128)S(1)}, u32[]{:S(2)}, u32[]{:S(2)}) collective-permute-start(f32[64,2048]{1,0:T(8,128)S(1)} %inverse.1.own_ref), channel_id=1, source_target_pairs={{0,12},{12,0},{24,36},{36,24},{48,60},{60,48},{72,84},{84,72},{96,... | collective-permute-start | bytes 1572872 | tf_op jit(solution)/shard_map/ppermute | solution.py:355
  44.7 12.3 %all-to-all-start.1 = ((f32[24,1,128]{2,1,0:T(1,128)}), f32[24,1,128]{2,1,0:T(1,128)S(1)}, u32[]{:S(2)}, u32[]{:S(2)}) async-start(f32[24,1,128]{2,1,0:T(1,128)} %bitcast.12), calls=%async_computation.1 | async-start | bytes 24576 | tf_op jit(solution)/shard_map/all_to_all | solution.py:344
  57.0 9.3 %all-to-all-done.1 = f32[24,1,128]{2,1,0:T(1,128)S(1)} async-done(((f32[24,1,128]{2,1,0:T(1,128)}), f32[24,1,128]{2,1,0:T(1,128)S(1)}, u32[]{:S(2)}, u32[]{:S(2)}) %all-to-all-start.1) | async-done | bytes 12320 | tf_op jit(solution)/shard_map/all_to_all | solution.py:344
  66.3 0.0 collective-permute-done.other_ref
  66.3 0.0 copy-done
  66.3 1.3 %weights.1 = f32[64,4096]{1,0:T(8,128)} custom-call(s32[1]{0:T(128)} %bitcast.6.core_ref, f32[24,128]{1,0:T(8,128)S(1)} %bitcast.17, f32[64,2048]{1,0:T(8,128)S(1)} %inverse.1.own_ref, f32[64,2048]{1,0:T(8,128)S(1)} %collective-permute-done.other_ref, f32[64,4096]{1,0:T(8,128)S(1)} %copy-done), custom_call_target="tpu_custom_call" | custom-call | tf_op jit(solution)/shard_map/weights/pallas_call | solution.py:357
Async XLA Ops:
  5.3 33.1 %all-to-all-start = ((f32[1088,1,128]{2,1,0:T(1,128)}), f32[1088,1,128]{2,1,0:T(1,128)S(1)}, u32[]{:S(2)}, u32[]{:S(2)}) async-start(f32[1088,1,128]{2,1,0:T(1,128)} %bitcast.9), calls=%async_computation | async-start | bytes 1114112 | tf_op jit(solution)/shard_map/all_to_all | solution.py:318
  38.4 2.9 %copy-start.1 = (bf16[576,256]{1,0:T(8,128)(2,1)S(1)}, bf16[576,256]{1,0:T(8,128)(2,1)}, u32[]{:S(2)}) copy-start(bf16[576,256]{1,0:T(8,128)(2,1)} %constant.15.clone.weights_ref) | copy-start | bytes 884740
  41.2 25.0 %copy-start = (f32[64,4096]{1,0:T(8,128)S(1)}, f32[64,4096]{1,0:T(8,128)}, u32[]{:S(2)}) copy-start(f32[64,4096]{1,0:T(8,128)} %weights_ref.2) | copy-start | bytes 3145732
  42.4 23.9 %collective-permute-start = (f32[64,2048]{1,0:T(8,128)S(1)}, f32[64,2048]{1,0:T(8,128)S(1)}, u32[]{:S(2)}, u32[]{:S(2)}) collective-permute-start(f32[64,2048]{1,0:T(8,128)S(1)} %inverse.1.own_ref), channel_id=1, source_target_pairs={{0,12},{12,0},{24,36},{36,24},{48,60},{60,48},{72,84},{84,72},{96,... | collective-permute-start | bytes 1572872 | tf_op jit(solution)/shard_map/ppermute | solution.py:355
  44.7 21.5 %all-to-all-start.1 = ((f32[24,1,128]{2,1,0:T(1,128)}), f32[24,1,128]{2,1,0:T(1,128)S(1)}, u32[]{:S(2)}, u32[]{:S(2)}) async-start(f32[24,1,128]{2,1,0:T(1,128)} %bitcast.12), calls=%async_computation.1 | async-start | bytes 24576 | tf_op jit(solution)/shard_map/all_to_all | solution.py:344

commit v3 on v2

--- a/solution.py
+++ b/solution.py
@@ -44,8 +44,9 @@
 
 
 def scatter_weights(mat):
-    perm = np.arange(GROUP).reshape(SIDE, BLOCK).T.reshape(-1)
-    return right_weights(mat[perm])
+    four = np.kron(np.eye(4, dtype=np.float32), mat)
+    order = np.arange(QUAD).reshape(4, SIDE, BLOCK).transpose(2, 0, 1).reshape(-1)
+    return np.stack(halves(four[order]))
 
 
 def iota(shape, axis):
@@ -103,22 +104,18 @@
 
 def send_kernel(mom_hbm, grad_hbm, picks_hbm, counts_hbm, weights_hbm, send_ref,
                 mom_ref, grad_ref, picks_ref, counts_ref, weights_ref, sems):
-    copies = [
-        pltpu.make_async_copy(src, dst, sems.at[i])
-        for i, (src, dst) in enumerate((
-            (picks_hbm, picks_ref), (counts_hbm, counts_ref), (weights_hbm, weights_ref),
-            (mom_hbm, mom_ref), (grad_hbm, grad_ref)))
-    ]
+    width = mom_ref.shape[1]
+    pairs = ((picks_hbm, picks_ref), (counts_hbm, counts_ref), (weights_hbm, weights_ref),
+             (mom_hbm, mom_ref), (grad_hbm, grad_ref))
+    copies = [pltpu.make_async_copy(src, dst, sems.at[i]) for i, (src, dst) in enumerate(pairs)]
     for copy in copies:
         copy.start()
-    width = mom_ref.shape[1]
-    quads = width // QUAD
 
     row = iota((QUAD, 128), 0)
     lane = iota((QUAD, 128), 1)
     pack = flag((row // GROUP == (lane // 16) % 4) & (row % BLOCK == (lane // BLOCK) % BLOCK))
-    row = iota((8, 384), 0)
-    lane = iota((8, 384), 1)
+    row = iota((8, 256), 0)
+    lane = iota((8, 256), 1)
     fold = flag((row // KMAX == (lane % 128) // 64) & (row % KMAX == (lane // 8) % KMAX))
     row = iota((128, 128), 0)
     lane = iota((128, 128), 1)
@@ -131,34 +128,32 @@
     groups = picks.shape[1]
     wide = spread_lanes(picks, width, 0)
     weights = weights_ref[...]
+
     for copy in copies[3:]:
         copy.wait()
+
     moment = 0.9 * mom_ref[...] + grad_ref[...].astype(F32)
     coef = times_right(stack_quads(times_left(weights[:GROUP], moment)), weights)
-    packed = []
-    for first in range(0, quads, 4):
+    done = []
+    for first in range(0, width // QUAD, 4):
         parts = []
         for q in range(first, first + 4):
             quad = coef[q * GROUP : (q + 1) * GROUP]
             for k in range(KMAX):
-                chosen = jnp.where(number == wide[k : k + 1, q * QUAD : (q + 1) * QUAD], quad, 0.0)
-                some = chosen[:8]
-                for b in range(1, GROUP // 8):
-                    some = some + chosen[b * 8 : (b + 1) * 8]
+                pick = wide[k : k + 1, q * QUAD : (q + 1) * QUAD]
+                some = jnp.zeros((8, QUAD), F32)
+                for b in range(GROUP // 8):
+                    rows = slice(b * 8, (b + 1) * 8)
+                    some = jnp.where(number[rows] == pick, quad[rows], some)
                 parts.append(some)
-        some = jnp.concatenate(parts, axis=0)
-        high = some.astype(BF16)
-        rest = some - high.astype(F32)
-        mid = rest.astype(BF16)
-        low = (rest - mid.astype(F32)).astype(BF16)
-        lanes = dot(jnp.concatenate([high, mid, low], axis=0), pack)
-        lanes = jnp.concatenate([jnp.where(fits, lanes[t * 128 : (t + 1) * 128], 0.0) for t in range(3)], axis=0)
-        packed.append(dot(fold, lanes.astype(BF16)))
+        lanes = dot(jnp.concatenate(split(jnp.concatenate(parts, axis=0)), axis=0), pack)
+        lanes = jnp.concatenate([jnp.where(fits, lanes[t * 128 : (t + 1) * 128], 0.0) for t in range(2)], axis=0)
+        done.append(dot(fold, lanes.astype(BF16)))
     part = groups // 2
     both = []
     for h in range(2):
         row = jnp.concatenate([picks[k : k + 1, h * part : (h + 1) * part] for k in range(KMAX)], axis=1)
-        both += [packed[2 * h], packed[2 * h + 1], row]
+        both += [done[2 * h], done[2 * h + 1], row]
     again = jnp.concatenate(both * 4, axis=0)
     for d in range(send_ref.shape[0] // again.shape[0]):
         send_ref[d * again.shape[0] : (d + 1) * again.shape[0], :] = again
@@ -213,11 +208,8 @@
         high_ref[t] = high
         low_ref[t] = low
 
-    slot_of_lane = (iota((8, QUAD), 1) // SIDE) % BLOCK
-    slot_of_row = iota((8, QUAD), 0) // BLOCK
-    in_low = slot_of_lane == slot_of_row
-    in_high = slot_of_lane == slot_of_row + 2
-    upper = iota((8, QUAD), 0) < BLOCK
+    upper = iota((8, 128), 0) < BLOCK
+    early = iota((8, 128), 1) < GROUP
     block_of_row = iota((GROUP, QUAD), 0).astype(F32)
 
     def eight(t, energy):
@@ -225,57 +217,54 @@
         rows8 = rows_ref[pl.ds(base, 8), :]
         cols8 = cols_ref[pl.ds(base, 8), :]
         for g in range(8):
-            vals = [high_ref[t, g * 16 : (g + 1) * 16, :].astype(F32),
-                    low_ref[t, g * 16 : (g + 1) * 16, :].astype(F32)]
-            row = rows8[g : g + 1]
-            left = jnp.concatenate([
-                jnp.where(row == float(b), v, 0.0).astype(BF16) for b in range(4) for v in vals
-            ], axis=0)
+            vals = [high_ref[t, g * 16 : (g + 1) * 16, :], low_ref[t, g * 16 : (g + 1) * 16, :]]
+            row = jnp.broadcast_to(rows8[g : g + 1], (16, QUAD))
+            masks = [flag(row == float(b)) for b in range(4)]
+            left = jnp.concatenate([m * v for m in masks for v in vals], axis=0)
             onehot = flag(block_of_row == cols8[g : g + 1])
-            right = jnp.concatenate([onehot[b * 16 : (b + 1) * 16] for b in range(4) for _ in range(BLOCK)], axis=0)
+            right = jnp.concatenate([onehot, onehot], axis=0)
             out = lax.dot_general(left, right, (((1,), (1,)), ((), ())), preferred_element_type=F32)
-            folded = []
-            for b in range(4):
-                both = out[b * 32 : b * 32 + 16] + out[b * 32 + 16 : b * 32 + 32]
-                lanes = jnp.where(in_low, both[:8], jnp.where(in_high, both[8:], 0.0))
-                folded.append(lanes + pltpu.roll(lanes, 4, 0))
+            both = [out[b * 32 : b * 32 + 16] + out[b * 32 + 16 : b * 32 + 32] for b in range(4)]
             for b in range(0, 4, 2):
-                coef = jnp.where(upper, folded[b], folded[b + 1])
-                coef_ref[pl.ds(pl.multiple_of(t * 128 + g * 16 + b * 4, 8), 8), :] = coef
-                energy = energy + coef * coef
+                for j in range(2):
+                    one, two = both[b][j * 8 : j * 8 + 8], both[b + 1][j * 8 : j * 8 + 8]
+                    first = jnp.where(upper, one, pltpu.roll(two, BLOCK, 0))
+                    second = jnp.where(upper, pltpu.roll(one, BLOCK, 0), two)
+                    coef = jnp.where(early, first, second)
+                    coef_ref[pl.ds(pl.multiple_of(t * 128 + g * 16 + b * 4, 8), 8), j * 128 : (j + 1) * 128] = coef
+                    energy = energy + coef * coef
         return energy
 
-    energy = lax.fori_loop(0, eights, eight, jnp.zeros((8, QUAD), F32))
-    energy = jnp.sum(energy[:, :128] + energy[:, 128:], axis=0, keepdims=True)
+    energy = lax.fori_loop(0, eights, eight, jnp.zeros((8, 128), F32), unroll=True)
+    energy = jnp.sum(energy, axis=0, keepdims=True)
     energy_ref[...] = jnp.broadcast_to(energy, energy_ref.shape)
 
 
-def inverse_kernel(coef_ref, weights_ref, update_ref, wide_ref):
+def inverse_kernel(core_ref, own_ref, other_ref, weights_ref, update_ref, wide_ref):
     weights = weights_ref[...]
     half_lane = iota((16, 128), 1) < GROUP
-    for t in range(coef_ref.shape[0] // QUAD):
-        back = times_right(coef_ref[t * QUAD : (t + 1) * QUAD, :], weights)
-        for pair in range(8):
-            even = back[pair * 32 : pair * 32 + 16]
-            odd = back[pair * 32 + 16 : pair * 32 + 32]
-            lanes = slice((t * 8 + pair) * 128, (t * 8 + pair + 1) * 128)
-            for w in range(2):
-                e = even[:, w * 128 : (w + 1) * 128]
-                o = odd[:, w * 128 : (w + 1) * 128]
-                wide_ref[w * 32 : w * 32 + 16, lanes] = jnp.where(half_lane, e, pltpu.roll(o, GROUP, 1))
-                wide_ref[w * 32 + 16 : w * 32 + 32, lanes] = jnp.where(half_lane, pltpu.roll(e, GROUP, 1), o)
-        lanes = slice(t * 1024, (t + 1) * 1024)
-        update_ref[:, lanes] = times_left(weights[:GROUP], wide_ref[:, lanes])
-
-
-def weights_kernel(replicas, total_rows, core_ref, energy_ref, own_ref, other_ref, weights_ref, out_ref):
+    half = update_ref.shape[1] // 2
+    mine = core_ref[0] * half
+    for coef_ref, start in ((own_ref, mine), (other_ref, half - mine)):
+        for t in range(coef_ref.shape[0] // QUAD):
+            back = times_right(coef_ref[t * QUAD : (t + 1) * QUAD, :], weights)
+            for pair in range(8):
+                even = back[pair * 32 : pair * 32 + 16]
+                odd = back[pair * 32 + 16 : pair * 32 + 32]
+                lanes = slice(pair * 128, (pair + 1) * 128)
+                for w in range(2):
+                    e = even[:, w * 128 : (w + 1) * 128]
+                    o = odd[:, w * 128 : (w + 1) * 128]
+                    wide_ref[w * 32 : w * 32 + 16, lanes] = jnp.where(half_lane, e, pltpu.roll(o, GROUP, 1))
+                    wide_ref[w * 32 + 16 : w * 32 + 32, lanes] = jnp.where(half_lane, pltpu.roll(e, GROUP, 1), o)
+            update_ref[:, pl.ds(pl.multiple_of(start + t * 1024, 1024), 1024)] = times_left(
+                weights[:GROUP], wide_ref[...])
+
+
+def weights_kernel(replicas, total_rows, energy_ref, update_ref, weights_ref, out_ref):
     mean = jnp.broadcast_to(jnp.sum(energy_ref[...]) * (1.0 / (replicas * replicas * total_rows)), (8, 128))
     factor = ((0.5 / replicas) / jnp.sqrt(mean + 1e-06))[:1, :1]
-    half = own_ref.shape[1]
-    mine = core_ref[0] * half
-    for mult, ref in ((mine, own_ref), (half - mine, other_ref)):
-        cols = pl.ds(pl.multiple_of(mult, half), half)
-        out_ref[:, cols] = weights_ref[:, cols] - ref[...] * factor
+    out_ref[...] = weights_ref[...] - update_ref[...] * factor
 
 
 def whole(shape):
@@ -343,24 +332,24 @@
     partners = [[(2 * chip + core) * nmp + z for core in range(2) for z in range(nmp)] for chip in range(replicas // 2)]
     energies = lax.all_to_all(energy.reshape(2 * nmp, 1, 128), ("dp", "mp"), 0, 0, tiled=True,
                               axis_index_groups=partners).reshape(2 * nmp, 128)
-    own = pl.pallas_call(
+    other = lax.ppermute(coef, "dp", [(p, p ^ 1) for p in range(replicas)])
+    core = jnp.bitwise_and(lax.axis_index("dp"), 1).astype(jnp.int32).reshape(1)
+    update = pl.pallas_call(
         inverse_kernel,
-        out_shape=jax.ShapeDtypeStruct((GROUP, half), F32),
-        scratch_shapes=[pltpu.VMEM((GROUP, half), F32)],
-        compiler_params=PARAMS,
-        cost_estimate=pl.CostEstimate(flops=6 * 2 * GROUP * GROUP * half, bytes_accessed=8 * GROUP * half,
+        in_specs=[pl.BlockSpec(memory_space=pltpu.SMEM)] + [vmem] * 3,
+        out_shape=jax.ShapeDtypeStruct((GROUP, width), F32),
+        scratch_shapes=[pltpu.VMEM((GROUP, 1024), F32)],
+        compiler_params=PARAMS,
+        cost_estimate=pl.CostEstimate(flops=6 * 2 * 2 * GROUP * GROUP * width, bytes_accessed=8 * GROUP * width,
                                       transcendentals=0),
         name="inverse",
-    )(coef, scatter)
-    other = lax.ppermute(own, "dp", [(p, p ^ 1) for p in range(replicas)])
-    core = jnp.bitwise_and(lax.axis_index("dp"), 1).astype(jnp.int32).reshape(1)
+    )(core, coef, other, scatter)
     new_weights = pl.pallas_call(
         functools.partial(weights_kernel, float(replicas), float(GROUP * nmp * width)),
-        in_specs=[pl.BlockSpec(memory_space=pltpu.SMEM)] + [vmem] * 4,
         out_shape=jax.ShapeDtypeStruct((GROUP, width), F32),
         compiler_params=PARAMS,
         name="weights",
-    )(core, energies, own, other, weights)
+    )(energies, update, weights)
     return (new_momentum[None], new_weights)
 
 

time: 67.9 us -> 65.3 us (0.962)
  waiting for transfers between devices: 21.9 us -> 19.6 us
    all_to_all x1, waiting for transfers between devices: 9.26 us -> 7.02 us  [on_device(): lax.all_to_all(energy.reshape(2 * nmp, 1, 128), ('dp', 'mp'), 0, 0, tiled...]
    pallas_call x1, Pallas kernels: 2.85 us -> 1.62 us  [on_device(): pl.pallas_call(scatter_kernel, in_specs=[vmem, hbm], out_shape=[jax.Shape...]
    pallas_call x1, Pallas kernels: 1.16 us -> 2.2 us  [on_device(): pl.pallas_call(inverse_kernel, in_specs=[pl.BlockSpec(memory_space=pltpu....]
  transfers between devices with their start and end apart: 3 -> 3, of which waited for: 2 -> 2; matrix products, arithmetic and copies ran while one was open for 0% -> 0% of each run, Pallas kernels for 9% -> 13%
where the time goes in v3:
time: 65.3 us; the launch traced here: 64.9 us
  starting transfers between devices  29.2 us (45%)
  waiting for transfers between devices  19.6 us (30%)
  Pallas kernels  15.4 us (24%)
  between operations  0.7 us (1%)
    all_to_all x1, starting transfers between devices, on_device(): lax.all_to_all(send.reshape(replicas * ROWS, 1, 128), 'dp', 0, 0, tiled=T...  14.6 us
    all_to_all x1, waiting for transfers between devices, on_device(): lax.all_to_all(send.reshape(replicas * ROWS, 1, 128), 'dp', 0, 0, tiled=T...  12.6 us
    all_to_all x1, starting transfers between devices, on_device(): lax.all_to_all(energy.reshape(2 * nmp, 1, 128), ('dp', 'mp'), 0, 0, tiled...  12.3 us
    all_to_all x1, waiting for transfers between devices, on_device(): lax.all_to_all(energy.reshape(2 * nmp, 1, 128), ('dp', 'mp'), 0, 0, tiled...  7.02 us
    pallas_call x1, Pallas kernels, on_device(): pl.pallas_call(momentum_kernel, grid=(steps,), in_specs=[tile, tile, whol...  5.92 us
    pallas_call x1, Pallas kernels, on_device(): pl.pallas_call(send_kernel, in_specs=[hbm] * 5, out_shape=jax.ShapeDtypeS...  4.42 us
    ppermute x1, starting transfers between devices, on_device(): other = lax.ppermute(coef, 'dp', [(p, p ^ 1) for p in range(replicas)])  2.3 us
    pallas_call x1, Pallas kernels, on_device(): pl.pallas_call(inverse_kernel, in_specs=[pl.BlockSpec(memory_space=pltpu....  2.2 us
  transfers between devices with their start and end apart: 3, of which 2 were waited for; matrix products, arithmetic and copies ran while one was open for 0% of the time, Pallas kernels for 13%

profile of v3, /device:TPU:1, one launch (start us, length us, event | category | flops | bytes accessed | tf_op | source)
XLA Modules:
  0.0 64.9 jit_solution(3197514259050245212)
XLA Ops:
  0.6 4.4 %send.1 = f32[1088,128]{1,0:T(8,128)} custom-call(f32[64,4096]{1,0:T(8,128)} %bitcast.18, bf16[64,4096]{1,0:T(8,128)(2,1)} %bitcast.21, s32[4,64]{1,0:T(4,128)} %bitcast.23, s32[1,64]{1,0:T(1,128)} %bitcast.25, bf16[576,256]{1,0:T(8,128)(2,1)} %constant.13.clone.forward_ref.weights_hbm), custom_call_target="tpu_custom_call" | custom-call | tf_op jit(solution)/shard_map/send/pallas_call | solution.py:291
  5.1 14.6 %all-to-all-start = ((f32[1088,1,128]{2,1,0:T(1,128)}), f32[1088,1,128]{2,1,0:T(1,128)S(1)}, u32[]{:S(2)}, u32[]{:S(2)}) async-start(f32[1088,1,128]{2,1,0:T(1,128)} %bitcast.8), calls=%async_computation | async-start | bytes 1114112 | tf_op jit(solution)/shard_map/all_to_all | solution.py:307
  19.7 5.9 %momentum.1._ = f32[64,4096]{1,0:T(8,128)} custom-call(f32[64,4096]{1,0:T(8,128)} %bitcast.19, bf16[64,4096]{1,0:T(8,128)(2,1)} %bitcast.22, s32[4,64]{1,0:T(4,128)} %bitcast.24, s32[1,64]{1,0:T(1,128)} %bitcast.26, bf16[576,256]{1,0:T(8,128)(2,1)} %constant.13.clone.forward_ref.weights_hbm, bf16[576,256]{1,0:T(8,128)(2,1)} %constant.14.clone.inverse_ref), custom_call_target="tpu_custom_call" | custom-call | flops 805306368 | bytes 2621440 | tf_op jit(solution)/shard_map/momentum/pallas_call | solution.py:308
  25.6 12.6 %all-to-all-done = f32[1088,1,128]{2,1,0:T(1,128)S(1)} async-done(((f32[1088,1,128]{2,1,0:T(1,128)}), f32[1088,1,128]{2,1,0:T(1,128)S(1)}, u32[]{:S(2)}, u32[]{:S(2)}) %all-to-all-start) | async-done | bytes 557088 | tf_op jit(solution)/shard_map/all_to_all | solution.py:307
  38.2 0.0 copy-start.1
  38.2 1.6 %scatter.1 = (f32[512,256]{1,0:T(8,128)S(1)}, f32[24,128]{1,0:T(8,128)}) custom-call(f32[1088,128]{1,0:T(8,128)S(1)} %bitcast.16, f32[64,4096]{1,0:T(8,128)} %momentum.1._), custom_call_target="tpu_custom_call" | custom-call | tf_op jit(solution)/shard_map/scatter/pallas_call | solution.py:319
  39.8 2.3 %collective-permute-start = (f32[512,256]{1,0:T(8,128)S(1)}, f32[512,256]{1,0:T(8,128)S(1)}, u32[]{:S(2)}, u32[]{:S(2)}) collective-permute-start(f32[512,256]{1,0:T(8,128)S(1)} %get-tuple-element.5.own_ref), channel_id=1, source_target_pairs={{0,12},{12,0},{24,36},{36,24},{48,60},{60,48},{72,84},{84,72},{96,... | collective-permute-start | bytes 1572872 | tf_op jit(solution)/shard_map/ppermute | solution.py:335
  42.1 12.3 %all-to-all-start.1 = ((f32[24,1,128]{2,1,0:T(1,128)}), f32[24,1,128]{2,1,0:T(1,128)S(1)}, u32[]{:S(2)}, u32[]{:S(2)}) async-start(f32[24,1,128]{2,1,0:T(1,128)} %bitcast.11), calls=%async_computation.1 | async-start | bytes 24576 | tf_op jit(solution)/shard_map/all_to_all | solution.py:333
  54.4 0.0 collective-permute-done.other_ref
  54.4 0.0 copy-done.1
  54.4 0.0 copy-start
  54.4 2.2 %inverse.1.update_ref = f32[64,4096]{1,0:T(8,128)S(1)} custom-call(s32[1]{0:T(128)} %bitcast.13.core_ref, f32[512,256]{1,0:T(8,128)S(1)} %get-tuple-element.5.own_ref, f32[512,256]{1,0:T(8,128)S(1)} %collective-permute-done.other_ref, bf16[576,256]{1,0:T(8,128)(2,1)S(1)} %copy-done.1), custom_call_target="tpu_custom_call" | custom-call | flops 402653184 | bytes 2097152 | tf_op jit(solution)/shard_map/inverse/pallas_call | solution.py:337
  56.6 7.0 %all-to-all-done.1 = f32[24,1,128]{2,1,0:T(1,128)S(1)} async-done(((f32[24,1,128]{2,1,0:T(1,128)}), f32[24,1,128]{2,1,0:T(1,128)S(1)}, u32[]{:S(2)}, u32[]{:S(2)}) %all-to-all-start.1) | async-done | bytes 12320 | tf_op jit(solution)/shard_map/all_to_all | solution.py:333
  63.6 0.0 copy-done
  63.6 1.3 %weights.1 = f32[64,4096]{1,0:T(8,128)} custom-call(f32[24,128]{1,0:T(8,128)S(1)} %bitcast.17, f32[64,4096]{1,0:T(8,128)S(1)} %inverse.1.update_ref, f32[64,4096]{1,0:T(8,128)S(1)} %copy-done), custom_call_target="tpu_custom_call" | custom-call | tf_op jit(solution)/shard_map/weights/pallas_call | solution.py:347
Async XLA Ops:
  5.1 33.1 %all-to-all-start = ((f32[1088,1,128]{2,1,0:T(1,128)}), f32[1088,1,128]{2,1,0:T(1,128)S(1)}, u32[]{:S(2)}, u32[]{:S(2)}) async-start(f32[1088,1,128]{2,1,0:T(1,128)} %bitcast.8), calls=%async_computation | async-start | bytes 1114112 | tf_op jit(solution)/shard_map/all_to_all | solution.py:307
  38.2 16.2 %copy-start.1 = (bf16[576,256]{1,0:T(8,128)(2,1)S(1)}, bf16[576,256]{1,0:T(8,128)(2,1)}, u32[]{:S(2)}) copy-start(bf16[576,256]{1,0:T(8,128)(2,1)} %constant.15.clone.weights_ref) | copy-start | bytes 884740
  39.8 14.6 %collective-permute-start = (f32[512,256]{1,0:T(8,128)S(1)}, f32[512,256]{1,0:T(8,128)S(1)}, u32[]{:S(2)}, u32[]{:S(2)}) collective-permute-start(f32[512,256]{1,0:T(8,128)S(1)} %get-tuple-element.5.own_ref), channel_id=1, source_target_pairs={{0,12},{12,0},{24,36},{36,24},{48,60},{60,48},{72,84},{84,72},{96,... | collective-permute-start | bytes 1572872 | tf_op jit(solution)/shard_map/ppermute | solution.py:335
  42.1 21.5 %all-to-all-start.1 = ((f32[24,1,128]{2,1,0:T(1,128)}), f32[24,1,128]{2,1,0:T(1,128)S(1)}, u32[]{:S(2)}, u32[]{:S(2)}) async-start(f32[24,1,128]{2,1,0:T(1,128)} %bitcast.11), calls=%async_computation.1 | async-start | bytes 24576 | tf_op jit(solution)/shard_map/all_to_all | solution.py:333
  54.4 9.2 %copy-start = (f32[64,4096]{1,0:T(8,128)S(1)}, f32[64,4096]{1,0:T(8,128)}, u32[]{:S(2)}) copy-start(f32[64,4096]{1,0:T(8,128)} %weights_ref.2) | copy-start | bytes 3145732

commit v4 on v3

--- a/solution.py
+++ b/solution.py
@@ -102,6 +102,15 @@
     return dot(eight, member)
 
 
+def sums_of(tiles):
+    sub = iota(tiles[0].shape, 0)
+    for half in (4, 2, 1):
+        first = sub % (2 * half) < half
+        pairs = zip(tiles[:half], tiles[half:])
+        tiles = [jnp.where(first, a + pltpu.roll(a, 8 - half, 0), b + pltpu.roll(b, half, 0)) for a, b in pairs]
+    return tiles[0]
+
+
 def send_kernel(mom_hbm, grad_hbm, picks_hbm, counts_hbm, weights_hbm, send_ref,
                 mom_ref, grad_ref, picks_ref, counts_ref, weights_ref, sems):
     width = mom_ref.shape[1]
@@ -114,12 +123,10 @@
     row = iota((QUAD, 128), 0)
     lane = iota((QUAD, 128), 1)
     pack = flag((row // GROUP == (lane // 16) % 4) & (row % BLOCK == (lane // BLOCK) % BLOCK))
-    row = iota((8, 256), 0)
-    lane = iota((8, 256), 1)
-    fold = flag((row // KMAX == (lane % 128) // 64) & (row % KMAX == (lane // 8) % KMAX))
-    row = iota((128, 128), 0)
-    lane = iota((128, 128), 1)
-    fits = ((row % BLOCK) == (lane % BLOCK)) & (((row // 32) % 2) == (lane // 64))
+    sub = iota((8, 128), 0)
+    lane = iota((8, 128), 1)
+    fits = sub % BLOCK == lane % BLOCK
+    early = lane < GROUP
     number = numbers()
 
     for copy in copies[:3]:
@@ -134,21 +141,27 @@
 
     moment = 0.9 * mom_ref[...] + grad_ref[...].astype(F32)
     coef = times_right(stack_quads(times_left(weights[:GROUP], moment)), weights)
+    parts = []
+    for q in range(width // QUAD):
+        quad = coef[q * GROUP : (q + 1) * GROUP]
+        for k in range(KMAX):
+            pick = wide[k : k + 1, q * QUAD : (q + 1) * QUAD]
+            some = jnp.zeros((8, QUAD), F32)
+            for b in range(GROUP // 8):
+                rows = slice(b * 8, (b + 1) * 8)
+                some = jnp.where(number[rows] == pick, quad[rows], some)
+            parts.append(some)
+    lanes = dot(jnp.concatenate(split(jnp.concatenate(parts, axis=0)), axis=0), pack)
+    lanes = lanes[: lanes.shape[0] // 2] + lanes[lanes.shape[0] // 2 :]
     done = []
     for first in range(0, width // QUAD, 4):
-        parts = []
-        for q in range(first, first + 4):
-            quad = coef[q * GROUP : (q + 1) * GROUP]
+        rows = []
+        for q in (first, first + 2):
             for k in range(KMAX):
-                pick = wide[k : k + 1, q * QUAD : (q + 1) * QUAD]
-                some = jnp.zeros((8, QUAD), F32)
-                for b in range(GROUP // 8):
-                    rows = slice(b * 8, (b + 1) * 8)
-                    some = jnp.where(number[rows] == pick, quad[rows], some)
-                parts.append(some)
-        lanes = dot(jnp.concatenate(split(jnp.concatenate(parts, axis=0)), axis=0), pack)
-        lanes = jnp.concatenate([jnp.where(fits, lanes[t * 128 : (t + 1) * 128], 0.0) for t in range(2)], axis=0)
-        done.append(dot(fold, lanes.astype(BF16)))
+                at = (q * KMAX + k) * 8
+                two = lanes[at : at + 8], lanes[at + 32 : at + 40]
+                rows.append(jnp.where(fits, jnp.where(early, *two), 0.0))
+        done.append(sums_of(rows))
     part = groups // 2
     both = []
     for h in range(2):
@@ -261,10 +274,18 @@
                 weights[:GROUP], wide_ref[...])
 
 
-def weights_kernel(replicas, total_rows, energy_ref, update_ref, weights_ref, out_ref):
+def weights_kernel(replicas, total_rows, energy_ref, update_ref, weights_ref, out_hbm, out_ref, sems):
     mean = jnp.broadcast_to(jnp.sum(energy_ref[...]) * (1.0 / (replicas * replicas * total_rows)), (8, 128))
     factor = ((0.5 / replicas) / jnp.sqrt(mean + 1e-06))[:1, :1]
-    out_ref[...] = weights_ref[...] - update_ref[...] * factor
+    copies = []
+    part = out_ref.shape[0] // 4
+    for s in range(4):
+        rows = slice(s * part, (s + 1) * part)
+        out_ref[rows, :] = weights_ref[rows, :] - update_ref[rows, :] * factor
+        copies.append(pltpu.make_async_copy(out_ref.at[rows, :], out_hbm.at[rows, :], sems.at[s]))
+        copies[-1].start()
+    for copy in copies:
+        copy.wait()
 
 
 def whole(shape):
@@ -329,7 +350,7 @@
         compiler_params=PARAMS,
         name="scatter",
     )(got.reshape(replicas * ROWS, 128), pltpu.with_memory_space_constraint(new_momentum, pltpu.HBM))
-    partners = [[(2 * chip + core) * nmp + z for core in range(2) for z in range(nmp)] for chip in range(replicas // 2)]
+    partners = [[(2 * chip + core) * nmp + z for z in reversed(range(nmp)) for core in range(2)] for chip in range(replicas // 2)]
     energies = lax.all_to_all(energy.reshape(2 * nmp, 1, 128), ("dp", "mp"), 0, 0, tiled=True,
                               axis_index_groups=partners).reshape(2 * nmp, 128)
     other = lax.ppermute(coef, "dp", [(p, p ^ 1) for p in range(replicas)])
@@ -346,7 +367,10 @@
     )(core, coef, other, scatter)
     new_weights = pl.pallas_call(
         functools.partial(weights_kernel, float(replicas), float(GROUP * nmp * width)),
+        in_specs=[vmem] * 3,
+        out_specs=hbm,
         out_shape=jax.ShapeDtypeStruct((GROUP, width), F32),
+        scratch_shapes=[pltpu.VMEM((GROUP, width), F32), pltpu.SemaphoreType.DMA((4,))],
         compiler_params=PARAMS,
         name="weights",
     )(energies, update, weights)

time: 65.3 us -> 63.5 us (0.972)
  waiting for transfers between devices: 19.6 us -> 17.8 us
  Pallas kernels: 15.4 us -> 14.7 us
  starting transfers between devices: 29.2 us -> 29.9 us
    all_to_all x1, waiting for transfers between devices: 7.02 us -> 5.25 us  [on_device(): lax.all_to_all(energy.reshape(2 * nmp, 1, 128), ('dp', 'mp'), 0, 0, tiled...]
    all_to_all x1, starting transfers between devices: 12.3 us -> 13 us  [on_device(): lax.all_to_all(energy.reshape(2 * nmp, 1, 128), ('dp', 'mp'), 0, 0, tiled...]
where the time goes in v4:
time: 63.5 us; the launch traced here: 63.1 us
  starting transfers between devices  29.9 us (47%)
  waiting for transfers between devices  17.8 us (28%)
  Pallas kernels  14.7 us (23%)
  between operations  0.7 us (1%)
    all_to_all x1, starting transfers between devices, on_device(): lax.all_to_all(send.reshape(replicas * ROWS, 1, 128), 'dp', 0, 0, tiled=T...  14.6 us
    all_to_all x1, starting transfers between devices, on_device(): lax.all_to_all(energy.reshape(2 * nmp, 1, 128), ('dp', 'mp'), 0, 0, tiled...  13 us
    all_to_all x1, waiting for transfers between devices, on_device(): lax.all_to_all(send.reshape(replicas * ROWS, 1, 128), 'dp', 0, 0, tiled=T...  12.6 us
    pallas_call x1, Pallas kernels, on_device(): pl.pallas_call(momentum_kernel, grid=(steps,), in_specs=[tile, tile, whol...  5.92 us
    all_to_all x1, waiting for transfers between devices, on_device(): lax.all_to_all(energy.reshape(2 * nmp, 1, 128), ('dp', 'mp'), 0, 0, tiled...  5.25 us
    pallas_call x1, Pallas kernels, on_device(): pl.pallas_call(send_kernel, in_specs=[hbm] * 5, out_shape=jax.ShapeDtypeS...  3.77 us
    ppermute x1, starting transfers between devices, on_device(): other = lax.ppermute(coef, 'dp', [(p, p ^ 1) for p in range(replicas)])  2.3 us
    pallas_call x1, Pallas kernels, on_device(): pl.pallas_call(inverse_kernel, in_specs=[pl.BlockSpec(memory_space=pltpu....  2.2 us
  transfers between devices with their start and end apart: 3, of which 2 were waited for; matrix products, arithmetic and copies ran while one was open for 0% of the time, Pallas kernels for 13%

profile of v4, /device:TPU:1, one launch (start us, length us, event | category | flops | bytes accessed | tf_op | source)
XLA Modules:
  0.0 63.1 jit_solution(8053066076814538862)
XLA Ops:
  0.6 3.8 %send.1 = f32[1088,128]{1,0:T(8,128)} custom-call(f32[64,4096]{1,0:T(8,128)} %bitcast.18, bf16[64,4096]{1,0:T(8,128)(2,1)} %bitcast.21, s32[4,64]{1,0:T(4,128)} %bitcast.23, s32[1,64]{1,0:T(1,128)} %bitcast.25, bf16[576,256]{1,0:T(8,128)(2,1)} %constant.13.clone.forward_ref.weights_hbm), custom_call_target="tpu_custom_call" | custom-call | tf_op jit(solution)/shard_map/send/pallas_call | solution.py:312
  4.4 14.6 %all-to-all-start = ((f32[1088,1,128]{2,1,0:T(1,128)}), f32[1088,1,128]{2,1,0:T(1,128)S(1)}, u32[]{:S(2)}, u32[]{:S(2)}) async-start(f32[1088,1,128]{2,1,0:T(1,128)} %bitcast.8), calls=%async_computation | async-start | bytes 1114112 | tf_op jit(solution)/shard_map/all_to_all | solution.py:328
  19.0 5.9 %momentum.1._ = f32[64,4096]{1,0:T(8,128)} custom-call(f32[64,4096]{1,0:T(8,128)} %bitcast.19, bf16[64,4096]{1,0:T(8,128)(2,1)} %bitcast.22, s32[4,64]{1,0:T(4,128)} %bitcast.24, s32[1,64]{1,0:T(1,128)} %bitcast.26, bf16[576,256]{1,0:T(8,128)(2,1)} %constant.13.clone.forward_ref.weights_hbm, bf16[576,256]{1,0:T(8,128)(2,1)} %constant.14.clone.inverse_ref), custom_call_target="tpu_custom_call" | custom-call | flops 805306368 | bytes 2621440 | tf_op jit(solution)/shard_map/momentum/pallas_call | solution.py:329
  24.9 12.6 %all-to-all-done = f32[1088,1,128]{2,1,0:T(1,128)S(1)} async-done(((f32[1088,1,128]{2,1,0:T(1,128)}), f32[1088,1,128]{2,1,0:T(1,128)S(1)}, u32[]{:S(2)}, u32[]{:S(2)}) %all-to-all-start) | async-done | bytes 557088 | tf_op jit(solution)/shard_map/all_to_all | solution.py:328
  37.5 0.0 copy-start.1
  37.5 1.6 %scatter.1 = (f32[512,256]{1,0:T(8,128)S(1)}, f32[24,128]{1,0:T(8,128)}) custom-call(f32[1088,128]{1,0:T(8,128)S(1)} %bitcast.16, f32[64,4096]{1,0:T(8,128)} %momentum.1._), custom_call_target="tpu_custom_call" | custom-call | tf_op jit(solution)/shard_map/scatter/pallas_call | solution.py:340
  39.2 2.3 %collective-permute-start = (f32[512,256]{1,0:T(8,128)S(1)}, f32[512,256]{1,0:T(8,128)S(1)}, u32[]{:S(2)}, u32[]{:S(2)}) collective-permute-start(f32[512,256]{1,0:T(8,128)S(1)} %get-tuple-element.5.own_ref), channel_id=1, source_target_pairs={{0,12},{12,0},{24,36},{36,24},{48,60},{60,48},{72,84},{84,72},{96,... | collective-permute-start | bytes 1572872 | tf_op jit(solution)/shard_map/ppermute | solution.py:356
  41.5 13.0 %all-to-all-start.1 = ((f32[24,1,128]{2,1,0:T(1,128)}), f32[24,1,128]{2,1,0:T(1,128)S(1)}, u32[]{:S(2)}, u32[]{:S(2)}) async-start(f32[24,1,128]{2,1,0:T(1,128)} %bitcast.11), calls=%async_computation.1 | async-start | bytes 24576 | tf_op jit(solution)/shard_map/all_to_all | solution.py:354
  54.5 0.0 collective-permute-done.other_ref
  54.5 0.0 copy-done.1
  54.5 0.0 copy-start
  54.5 2.2 %inverse.1.update_ref = f32[64,4096]{1,0:T(8,128)S(1)} custom-call(s32[1]{0:T(128)} %bitcast.13.core_ref, f32[512,256]{1,0:T(8,128)S(1)} %get-tuple-element.5.own_ref, f32[512,256]{1,0:T(8,128)S(1)} %collective-permute-done.other_ref, bf16[576,256]{1,0:T(8,128)(2,1)S(1)} %copy-done.1), custom_call_target="tpu_custom_call" | custom-call | flops 402653184 | bytes 2097152 | tf_op jit(solution)/shard_map/inverse/pallas_call | solution.py:358
  56.7 5.3 %all-to-all-done.1 = f32[24,1,128]{2,1,0:T(1,128)S(1)} async-done(((f32[24,1,128]{2,1,0:T(1,128)}), f32[24,1,128]{2,1,0:T(1,128)S(1)}, u32[]{:S(2)}, u32[]{:S(2)}) %all-to-all-start.1) | async-done | bytes 12320 | tf_op jit(solution)/shard_map/all_to_all | solution.py:354
  62.0 0.0 copy-done
  62.0 1.2 %weights.1 = f32[64,4096]{1,0:T(8,128)} custom-call(f32[24,128]{1,0:T(8,128)S(1)} %bitcast.17, f32[64,4096]{1,0:T(8,128)S(1)} %inverse.1.update_ref, f32[64,4096]{1,0:T(8,128)S(1)} %copy-done), custom_call_target="tpu_custom_call" | custom-call | tf_op jit(solution)/shard_map/weights/pallas_call | solution.py:368
Async XLA Ops:
  4.4 33.1 %all-to-all-start = ((f32[1088,1,128]{2,1,0:T(1,128)}), f32[1088,1,128]{2,1,0:T(1,128)S(1)}, u32[]{:S(2)}, u32[]{:S(2)}) async-start(f32[1088,1,128]{2,1,0:T(1,128)} %bitcast.8), calls=%async_computation | async-start | bytes 1114112 | tf_op jit(solution)/shard_map/all_to_all | solution.py:328
  37.5 16.9 %copy-start.1 = (bf16[576,256]{1,0:T(8,128)(2,1)S(1)}, bf16[576,256]{1,0:T(8,128)(2,1)}, u32[]{:S(2)}) copy-start(bf16[576,256]{1,0:T(8,128)(2,1)} %constant.15.clone.weights_ref) | copy-start | bytes 884740
  39.2 15.3 %collective-permute-start = (f32[512,256]{1,0:T(8,128)S(1)}, f32[512,256]{1,0:T(8,128)S(1)}, u32[]{:S(2)}, u32[]{:S(2)}) collective-permute-start(f32[512,256]{1,0:T(8,128)S(1)} %get-tuple-element.5.own_ref), channel_id=1, source_target_pairs={{0,12},{12,0},{24,36},{36,24},{48,60},{60,48},{72,84},{84,72},{96,... | collective-permute-start | bytes 1572872 | tf_op jit(solution)/shard_map/ppermute | solution.py:356
  41.5 20.5 %all-to-all-start.1 = ((f32[24,1,128]{2,1,0:T(1,128)}), f32[24,1,128]{2,1,0:T(1,128)S(1)}, u32[]{:S(2)}, u32[]{:S(2)}) async-start(f32[24,1,128]{2,1,0:T(1,128)} %bitcast.11), calls=%async_computation.1 | async-start | bytes 24576 | tf_op jit(solution)/shard_map/all_to_all | solution.py:354
  54.5 7.5 %copy-start = (f32[64,4096]{1,0:T(8,128)S(1)}, f32[64,4096]{1,0:T(8,128)}, u32[]{:S(2)}) copy-start(f32[64,4096]{1,0:T(8,128)} %weights_ref.2) | copy-start | bytes 3145732

commit v5 on v4

--- a/solution.py
+++ b/solution.py
@@ -243,7 +243,7 @@
                     one, two = both[b][j * 8 : j * 8 + 8], both[b + 1][j * 8 : j * 8 + 8]
                     first = jnp.where(upper, one, pltpu.roll(two, BLOCK, 0))
                     second = jnp.where(upper, pltpu.roll(one, BLOCK, 0), two)
-                    coef = jnp.where(early, first, second)
+                    coef = jnp.where(early, first, second) * (1.0 / replicas)
                     coef_ref[pl.ds(pl.multiple_of(t * 128 + g * 16 + b * 4, 8), 8), j * 128 : (j + 1) * 128] = coef
                     energy = energy + coef * coef
         return energy
@@ -274,9 +274,9 @@
                 weights[:GROUP], wide_ref[...])
 
 
-def weights_kernel(replicas, total_rows, energy_ref, update_ref, weights_ref, out_hbm, out_ref, sems):
-    mean = jnp.broadcast_to(jnp.sum(energy_ref[...]) * (1.0 / (replicas * replicas * total_rows)), (8, 128))
-    factor = ((0.5 / replicas) / jnp.sqrt(mean + 1e-06))[:1, :1]
+def weights_kernel(elements, energy_ref, update_ref, weights_ref, out_hbm, out_ref, sems):
+    mean = jnp.broadcast_to(jnp.sum(energy_ref[...]) * (1.0 / elements), (8, 128))
+    factor = (0.5 / jnp.sqrt(mean + 1e-06))[:1, :1]
     copies = []
     part = out_ref.shape[0] // 4
     for s in range(4):
@@ -325,7 +325,8 @@
         name="send",
     )(*taken)
 
-    got = lax.all_to_all(send.reshape(replicas * ROWS, 1, 128), "dp", 0, 0, tiled=True)
+    order = [[(replicas // 2 + 4 + p) % replicas for p in range(replicas)]]
+    got = lax.all_to_all(send.reshape(replicas * ROWS, 1, 128), "dp", 0, 0, tiled=True, axis_index_groups=order)
     new_momentum = pl.pallas_call(
         momentum_kernel,
         grid=(steps,),
@@ -366,7 +367,7 @@
         name="inverse",
     )(core, coef, other, scatter)
     new_weights = pl.pallas_call(
-        functools.partial(weights_kernel, float(replicas), float(GROUP * nmp * width)),
+        functools.partial(weights_kernel, float(GROUP * nmp * width)),
         in_specs=[vmem] * 3,
         out_specs=hbm,
         out_shape=jax.ShapeDtypeStruct((GROUP, width), F32),

time: 63.5 us -> 60.1 us (0.946)
  waiting for transfers between devices: 17.8 us -> 12.4 us
  starting transfers between devices: 29.9 us -> 32.1 us
    all_to_all x1, starting transfers between devices: 14.6 us -> 20.4 us  [on_device(): lax.all_to_all(send.reshape(replicas * ROWS, 1, 128), 'dp', 0, 0, tiled=T...]
    all_to_all x1, waiting for transfers between devices: 12.6 us -> 7.1 us  [on_device(): lax.all_to_all(send.reshape(replicas * ROWS, 1, 128), 'dp', 0, 0, tiled=T...]
    all_to_all x1, starting transfers between devices: 13 us -> 9.3 us  [on_device(): lax.all_to_all(energy.reshape(2 * nmp, 1, 128), ('dp', 'mp'), 0, 0, tiled...]
  transfers between devices with their start and end apart: 3 -> 3, of which waited for: 2 -> 2; matrix products, arithmetic and copies ran while one was open for 0% -> 0% of each run, Pallas kernels for 13% -> 14%
where the time goes in v5:
time: 60.1 us; the launch traced here: 59.8 us
  starting transfers between devices  32.1 us (53%)
  Pallas kernels  14.7 us (24%)
  waiting for transfers between devices  12.4 us (21%)
  between operations  0.7 us (1%)
    all_to_all x1, starting transfers between devices, on_device(): lax.all_to_all(send.reshape(replicas * ROWS, 1, 128), 'dp', 0, 0, tiled=T...  20.4 us
    all_to_all x1, starting transfers between devices, on_device(): lax.all_to_all(energy.reshape(2 * nmp, 1, 128), ('dp', 'mp'), 0, 0, tiled...  9.3 us
    all_to_all x1, waiting for transfers between devices, on_device(): lax.all_to_all(send.reshape(replicas * ROWS, 1, 128), 'dp', 0, 0, tiled=T...  7.1 us
    pallas_call x1, Pallas kernels, on_device(): pl.pallas_call(momentum_kernel, grid=(steps,), in_specs=[tile, tile, whol...  5.92 us
    all_to_all x1, waiting for transfers between devices, on_device(): lax.all_to_all(energy.reshape(2 * nmp, 1, 128), ('dp', 'mp'), 0, 0, tiled...  5.25 us
    pallas_call x1, Pallas kernels, on_device(): pl.pallas_call(send_kernel, in_specs=[hbm] * 5, out_shape=jax.ShapeDtypeS...  3.77 us
    ppermute x1, starting transfers between devices, on_device(): other = lax.ppermute(coef, 'dp', [(p, p ^ 1) for p in range(replicas)])  2.34 us
    pallas_call x1, Pallas kernels, on_device(): pl.pallas_call(inverse_kernel, in_specs=[pl.BlockSpec(memory_space=pltpu....  2.2 us
  transfers between devices with their start and end apart: 3, of which 2 were waited for; matrix products, arithmetic and copies ran while one was open for 0% of the time, Pallas kernels for 14%

profile of v5, /device:TPU:1, one launch (start us, length us, event | category | flops | bytes accessed | tf_op | source)
XLA Modules:
  0.0 59.8 jit_solution(16327303137147595675)
XLA Ops:
  0.6 3.8 %send.1 = f32[1088,128]{1,0:T(8,128)} custom-call(f32[64,4096]{1,0:T(8,128)} %bitcast.18, bf16[64,4096]{1,0:T(8,128)(2,1)} %bitcast.21, s32[4,64]{1,0:T(4,128)} %bitcast.23, s32[1,64]{1,0:T(1,128)} %bitcast.25, bf16[576,256]{1,0:T(8,128)(2,1)} %constant.13.clone.forward_ref.weights_hbm), custom_call_target="tpu_custom_call" | custom-call | tf_op jit(solution)/shard_map/send/pallas_call | solution.py:312
  4.4 20.4 %all-to-all-start = ((f32[1088,1,128]{2,1,0:T(1,128)}), f32[1088,1,128]{2,1,0:T(1,128)S(1)}, u32[]{:S(2)}, u32[]{:S(2)}) async-start(f32[1088,1,128]{2,1,0:T(1,128)} %bitcast.8), calls=%async_computation | async-start | bytes 1114112 | tf_op jit(solution)/shard_map/all_to_all | solution.py:329
  24.8 5.9 %momentum.1._ = f32[64,4096]{1,0:T(8,128)} custom-call(f32[64,4096]{1,0:T(8,128)} %bitcast.19, bf16[64,4096]{1,0:T(8,128)(2,1)} %bitcast.22, s32[4,64]{1,0:T(4,128)} %bitcast.24, s32[1,64]{1,0:T(1,128)} %bitcast.26, bf16[576,256]{1,0:T(8,128)(2,1)} %constant.13.clone.forward_ref.weights_hbm, bf16[576,256]{1,0:T(8,128)(2,1)} %constant.14.clone.inverse_ref), custom_call_target="tpu_custom_call" | custom-call | flops 805306368 | bytes 2621440 | tf_op jit(solution)/shard_map/momentum/pallas_call | solution.py:330
  30.8 7.1 %all-to-all-done = f32[1088,1,128]{2,1,0:T(1,128)S(1)} async-done(((f32[1088,1,128]{2,1,0:T(1,128)}), f32[1088,1,128]{2,1,0:T(1,128)S(1)}, u32[]{:S(2)}, u32[]{:S(2)}) %all-to-all-start) | async-done | bytes 557088 | tf_op jit(solution)/shard_map/all_to_all | solution.py:329
  37.9 0.0 copy-start.1
  37.9 1.6 %scatter.1 = (f32[512,256]{1,0:T(8,128)S(1)}, f32[24,128]{1,0:T(8,128)}) custom-call(f32[1088,128]{1,0:T(8,128)S(1)} %bitcast.16, f32[64,4096]{1,0:T(8,128)} %momentum.1._), custom_call_target="tpu_custom_call" | custom-call | tf_op jit(solution)/shard_map/scatter/pallas_call | solution.py:341
  39.5 2.3 %collective-permute-start = (f32[512,256]{1,0:T(8,128)S(1)}, f32[512,256]{1,0:T(8,128)S(1)}, u32[]{:S(2)}, u32[]{:S(2)}) collective-permute-start(f32[512,256]{1,0:T(8,128)S(1)} %get-tuple-element.5.own_ref), channel_id=1, source_target_pairs={{0,12},{12,0},{24,36},{36,24},{48,60},{60,48},{72,84},{84,72},{96,... | collective-permute-start | bytes 1572872 | tf_op jit(solution)/shard_map/ppermute | solution.py:357
  41.8 9.3 %all-to-all-start.1 = ((f32[24,1,128]{2,1,0:T(1,128)}), f32[24,1,128]{2,1,0:T(1,128)S(1)}, u32[]{:S(2)}, u32[]{:S(2)}) async-start(f32[24,1,128]{2,1,0:T(1,128)} %bitcast.11), calls=%async_computation.1 | async-start | bytes 24576 | tf_op jit(solution)/shard_map/all_to_all | solution.py:355
  51.1 0.0 collective-permute-done.other_ref
  51.1 0.0 copy-done.1
  51.1 0.0 copy-start
  51.2 2.2 %inverse.1.update_ref = f32[64,4096]{1,0:T(8,128)S(1)} custom-call(s32[1]{0:T(128)} %bitcast.13.core_ref, f32[512,256]{1,0:T(8,128)S(1)} %get-tuple-element.5.own_ref, f32[512,256]{1,0:T(8,128)S(1)} %collective-permute-done.other_ref, bf16[576,256]{1,0:T(8,128)(2,1)S(1)} %copy-done.1), custom_call_target="tpu_custom_call" | custom-call | flops 402653184 | bytes 2097152 | tf_op jit(solution)/shard_map/inverse/pallas_call | solution.py:359
  53.4 5.3 %all-to-all-done.1 = f32[24,1,128]{2,1,0:T(1,128)S(1)} async-done(((f32[24,1,128]{2,1,0:T(1,128)}), f32[24,1,128]{2,1,0:T(1,128)S(1)}, u32[]{:S(2)}, u32[]{:S(2)}) %all-to-all-start.1) | async-done | bytes 12320 | tf_op jit(solution)/shard_map/all_to_all | solution.py:355
  58.6 0.0 copy-done
  58.6 1.2 %weights.1 = f32[64,4096]{1,0:T(8,128)} custom-call(f32[24,128]{1,0:T(8,128)S(1)} %bitcast.17, f32[64,4096]{1,0:T(8,128)S(1)} %inverse.1.update_ref, f32[64,4096]{1,0:T(8,128)S(1)} %copy-done), custom_call_target="tpu_custom_call" | custom-call | tf_op jit(solution)/shard_map/weights/pallas_call | solution.py:369
Async XLA Ops:
  4.4 33.4 %all-to-all-start = ((f32[1088,1,128]{2,1,0:T(1,128)}), f32[1088,1,128]{2,1,0:T(1,128)S(1)}, u32[]{:S(2)}, u32[]{:S(2)}) async-start(f32[1088,1,128]{2,1,0:T(1,128)} %bitcast.8), calls=%async_computation | async-start | bytes 1114112 | tf_op jit(solution)/shard_map/all_to_all | solution.py:329
  37.9 13.3 %copy-start.1 = (bf16[576,256]{1,0:T(8,128)(2,1)S(1)}, bf16[576,256]{1,0:T(8,128)(2,1)}, u32[]{:S(2)}) copy-start(bf16[576,256]{1,0:T(8,128)(2,1)} %constant.15.clone.weights_ref) | copy-start | bytes 884740
  39.5 11.7 %collective-permute-start = (f32[512,256]{1,0:T(8,128)S(1)}, f32[512,256]{1,0:T(8,128)S(1)}, u32[]{:S(2)}, u32[]{:S(2)}) collective-permute-start(f32[512,256]{1,0:T(8,128)S(1)} %get-tuple-element.5.own_ref), channel_id=1, source_target_pairs={{0,12},{12,0},{24,36},{36,24},{48,60},{60,48},{72,84},{84,72},{96,... | collective-permute-start | bytes 1572872 | tf_op jit(solution)/shard_map/ppermute | solution.py:357
  41.8 16.8 %all-to-all-start.1 = ((f32[24,1,128]{2,1,0:T(1,128)}), f32[24,1,128]{2,1,0:T(1,128)S(1)}, u32[]{:S(2)}, u32[]{:S(2)}) async-start(f32[24,1,128]{2,1,0:T(1,128)} %bitcast.11), calls=%async_computation.1 | async-start | bytes 24576 | tf_op jit(solution)/shard_map/all_to_all | solution.py:355
  51.1 7.5 %copy-start = (f32[64,4096]{1,0:T(8,128)S(1)}, f32[64,4096]{1,0:T(8,128)}, u32[]{:S(2)}) copy-start(f32[64,4096]{1,0:T(8,128)} %weights_ref.2) | copy-start | bytes 3145732

commit v6 on v5

--- a/solution.py
+++ b/solution.py
@@ -325,7 +325,7 @@
         name="send",
     )(*taken)
 
-    order = [[(replicas // 2 + 4 + p) % replicas for p in range(replicas)]]
+    order = [[(replicas // 2 + 4 + 37 * p) % replicas for p in range(replicas)]]
     got = lax.all_to_all(send.reshape(replicas * ROWS, 1, 128), "dp", 0, 0, tiled=True, axis_index_groups=order)
     new_momentum = pl.pallas_call(
         momentum_kernel,

time: 60.1 us -> 59.6 us (level)
  waiting for transfers between devices: 12.4 us -> 11.7 us
    all_to_all x1, waiting for transfers between devices: 7.1 us -> 6.42 us  [on_device(): lax.all_to_all(send.reshape(replicas * ROWS, 1, 128), 'dp', 0, 0, tiled=T...]
where the time goes in v6:
time: 59.6 us; the launch traced here: 59.3 us
  starting transfers between devices  32.2 us (54%)
  Pallas kernels  14.7 us (25%)
  waiting for transfers between devices  11.7 us (20%)
  between operations  0.7 us (1%)
    all_to_all x1, starting transfers between devices, on_device(): lax.all_to_all(send.reshape(replicas * ROWS, 1, 128), 'dp', 0, 0, tiled=T...  20.4 us
    all_to_all x1, starting transfers between devices, on_device(): lax.all_to_all(energy.reshape(2 * nmp, 1, 128), ('dp', 'mp'), 0, 0, tiled...  9.26 us
    all_to_all x1, waiting for transfers between devices, on_device(): lax.all_to_all(send.reshape(replicas * ROWS, 1, 128), 'dp', 0, 0, tiled=T...  6.42 us
    pallas_call x1, Pallas kernels, on_device(): pl.pallas_call(momentum_kernel, grid=(steps,), in_specs=[tile, tile, whol...  5.92 us
    all_to_all x1, waiting for transfers between devices, on_device(): lax.all_to_all(energy.reshape(2 * nmp, 1, 128), ('dp', 'mp'), 0, 0, tiled...  5.25 us
    pallas_call x1, Pallas kernels, on_device(): pl.pallas_call(send_kernel, in_specs=[hbm] * 5, out_shape=jax.ShapeDtypeS...  3.77 us
    ppermute x1, starting transfers between devices, on_device(): other = lax.ppermute(coef, 'dp', [(p, p ^ 1) for p in range(replicas)])  2.59 us
    pallas_call x1, Pallas kernels, on_device(): pl.pallas_call(inverse_kernel, in_specs=[pl.BlockSpec(memory_space=pltpu....  2.2 us
  transfers between devices with their start and end apart: 3, of which 2 were waited for; matrix products, arithmetic and copies ran while one was open for 0% of the time, Pallas kernels for 14%

profile of v6, /device:TPU:1, one launch (start us, length us, event | category | flops | bytes accessed | tf_op | source)
XLA Modules:
  0.0 59.3 jit_solution(12027480075378952014)
XLA Ops:
  0.6 3.8 %send.1 = f32[1088,128]{1,0:T(8,128)} custom-call(f32[64,4096]{1,0:T(8,128)} %bitcast.18, bf16[64,4096]{1,0:T(8,128)(2,1)} %bitcast.21, s32[4,64]{1,0:T(4,128)} %bitcast.23, s32[1,64]{1,0:T(1,128)} %bitcast.25, bf16[576,256]{1,0:T(8,128)(2,1)} %constant.13.clone.forward_ref.weights_hbm), custom_call_target="tpu_custom_call" | custom-call | tf_op jit(solution)/shard_map/send/pallas_call | solution.py:312
  4.4 20.4 %all-to-all-start = ((f32[1088,1,128]{2,1,0:T(1,128)}), f32[1088,1,128]{2,1,0:T(1,128)S(1)}, u32[]{:S(2)}, u32[]{:S(2)}) async-start(f32[1088,1,128]{2,1,0:T(1,128)} %bitcast.8), calls=%async_computation | async-start | bytes 1114112 | tf_op jit(solution)/shard_map/all_to_all | solution.py:329
  24.8 5.9 %momentum.1._ = f32[64,4096]{1,0:T(8,128)} custom-call(f32[64,4096]{1,0:T(8,128)} %bitcast.19, bf16[64,4096]{1,0:T(8,128)(2,1)} %bitcast.22, s32[4,64]{1,0:T(4,128)} %bitcast.24, s32[1,64]{1,0:T(1,128)} %bitcast.26, bf16[576,256]{1,0:T(8,128)(2,1)} %constant.13.clone.forward_ref.weights_hbm, bf16[576,256]{1,0:T(8,128)(2,1)} %constant.14.clone.inverse_ref), custom_call_target="tpu_custom_call" | custom-call | flops 805306368 | bytes 2621440 | tf_op jit(solution)/shard_map/momentum/pallas_call | solution.py:330
  30.7 6.4 %all-to-all-done = f32[1088,1,128]{2,1,0:T(1,128)S(1)} async-done(((f32[1088,1,128]{2,1,0:T(1,128)}), f32[1088,1,128]{2,1,0:T(1,128)S(1)}, u32[]{:S(2)}, u32[]{:S(2)}) %all-to-all-start) | async-done | bytes 557088 | tf_op jit(solution)/shard_map/all_to_all | solution.py:329
  37.1 0.0 copy-start.1
  37.1 1.6 %scatter.1 = (f32[512,256]{1,0:T(8,128)S(1)}, f32[24,128]{1,0:T(8,128)}) custom-call(f32[1088,128]{1,0:T(8,128)S(1)} %bitcast.16, f32[64,4096]{1,0:T(8,128)} %momentum.1._), custom_call_target="tpu_custom_call" | custom-call | tf_op jit(solution)/shard_map/scatter/pallas_call | solution.py:341
  38.7 2.6 %collective-permute-start = (f32[512,256]{1,0:T(8,128)S(1)}, f32[512,256]{1,0:T(8,128)S(1)}, u32[]{:S(2)}, u32[]{:S(2)}) collective-permute-start(f32[512,256]{1,0:T(8,128)S(1)} %get-tuple-element.5.own_ref), channel_id=1, source_target_pairs={{0,12},{12,0},{24,36},{36,24},{48,60},{60,48},{72,84},{84,72},{96,... | collective-permute-start | bytes 1572872 | tf_op jit(solution)/shard_map/ppermute | solution.py:357
  41.3 9.3 %all-to-all-start.1 = ((f32[24,1,128]{2,1,0:T(1,128)}), f32[24,1,128]{2,1,0:T(1,128)S(1)}, u32[]{:S(2)}, u32[]{:S(2)}) async-start(f32[24,1,128]{2,1,0:T(1,128)} %bitcast.11), calls=%async_computation.1 | async-start | bytes 24576 | tf_op jit(solution)/shard_map/all_to_all | solution.py:355
  50.6 0.0 collective-permute-done.other_ref
  50.6 0.0 copy-done.1
  50.6 0.0 copy-start
  50.6 2.2 %inverse.1.update_ref = f32[64,4096]{1,0:T(8,128)S(1)} custom-call(s32[1]{0:T(128)} %bitcast.13.core_ref, f32[512,256]{1,0:T(8,128)S(1)} %get-tuple-element.5.own_ref, f32[512,256]{1,0:T(8,128)S(1)} %collective-permute-done.other_ref, bf16[576,256]{1,0:T(8,128)(2,1)S(1)} %copy-done.1), custom_call_target="tpu_custom_call" | custom-call | flops 402653184 | bytes 2097152 | tf_op jit(solution)/shard_map/inverse/pallas_call | solution.py:359
  52.8 5.2 %all-to-all-done.1 = f32[24,1,128]{2,1,0:T(1,128)S(1)} async-done(((f32[24,1,128]{2,1,0:T(1,128)}), f32[24,1,128]{2,1,0:T(1,128)S(1)}, u32[]{:S(2)}, u32[]{:S(2)}) %all-to-all-start.1) | async-done | bytes 12320 | tf_op jit(solution)/shard_map/all_to_all | solution.py:355
  58.1 0.0 copy-done
  58.1 1.2 %weights.1 = f32[64,4096]{1,0:T(8,128)} custom-call(f32[24,128]{1,0:T(8,128)S(1)} %bitcast.17, f32[64,4096]{1,0:T(8,128)S(1)} %inverse.1.update_ref, f32[64,4096]{1,0:T(8,128)S(1)} %copy-done), custom_call_target="tpu_custom_call" | custom-call | tf_op jit(solution)/shard_map/weights/pallas_call | solution.py:369
Async XLA Ops:
  4.4 32.7 %all-to-all-start = ((f32[1088,1,128]{2,1,0:T(1,128)}), f32[1088,1,128]{2,1,0:T(1,128)S(1)}, u32[]{:S(2)}, u32[]{:S(2)}) async-start(f32[1088,1,128]{2,1,0:T(1,128)} %bitcast.8), calls=%async_computation | async-start | bytes 1114112 | tf_op jit(solution)/shard_map/all_to_all | solution.py:329
  37.1 13.5 %copy-start.1 = (bf16[576,256]{1,0:T(8,128)(2,1)S(1)}, bf16[576,256]{1,0:T(8,128)(2,1)}, u32[]{:S(2)}) copy-start(bf16[576,256]{1,0:T(8,128)(2,1)} %constant.15.clone.weights_ref) | copy-start | bytes 884740
  38.7 11.9 %collective-permute-start = (f32[512,256]{1,0:T(8,128)S(1)}, f32[512,256]{1,0:T(8,128)S(1)}, u32[]{:S(2)}, u32[]{:S(2)}) collective-permute-start(f32[512,256]{1,0:T(8,128)S(1)} %get-tuple-element.5.own_ref), channel_id=1, source_target_pairs={{0,12},{12,0},{24,36},{36,24},{48,60},{60,48},{72,84},{84,72},{96,... | collective-permute-start | bytes 1572872 | tf_op jit(solution)/shard_map/ppermute | solution.py:357
  41.3 16.8 %all-to-all-start.1 = ((f32[24,1,128]{2,1,0:T(1,128)}), f32[24,1,128]{2,1,0:T(1,128)S(1)}, u32[]{:S(2)}, u32[]{:S(2)}) async-start(f32[24,1,128]{2,1,0:T(1,128)} %bitcast.11), calls=%async_computation.1 | async-start | bytes 24576 | tf_op jit(solution)/shard_map/all_to_all | solution.py:355
  50.6 7.5 %copy-start = (f32[64,4096]{1,0:T(8,128)S(1)}, f32[64,4096]{1,0:T(8,128)}, u32[]{:S(2)}) copy-start(f32[64,4096]{1,0:T(8,128)} %weights_ref.2) | copy-start | bytes 3145732

commit v7 on v6

--- a/solution.py
+++ b/solution.py
@@ -64,7 +64,7 @@
 
 def times_left(weights, x):
     high, low = split(x)
-    return dot(weights, jnp.concatenate([high, low, high, low], axis=0))
+    return dot(weights[:, : 3 * GROUP], jnp.concatenate([high, low, high], axis=0))
 
 
 def stack_quads(x):
@@ -278,8 +278,8 @@
     mean = jnp.broadcast_to(jnp.sum(energy_ref[...]) * (1.0 / elements), (8, 128))
     factor = (0.5 / jnp.sqrt(mean + 1e-06))[:1, :1]
     copies = []
-    part = out_ref.shape[0] // 4
-    for s in range(4):
+    part = out_ref.shape[0] // 8
+    for s in range(8):
         rows = slice(s * part, (s + 1) * part)
         out_ref[rows, :] = weights_ref[rows, :] - update_ref[rows, :] * factor
         copies.append(pltpu.make_async_copy(out_ref.at[rows, :], out_hbm.at[rows, :], sems.at[s]))
@@ -371,7 +371,7 @@
         in_specs=[vmem] * 3,
         out_specs=hbm,
         out_shape=jax.ShapeDtypeStruct((GROUP, width), F32),
-        scratch_shapes=[pltpu.VMEM((GROUP, width), F32), pltpu.SemaphoreType.DMA((4,))],
+        scratch_shapes=[pltpu.VMEM((GROUP, width), F32), pltpu.SemaphoreType.DMA((8,))],
         compiler_params=PARAMS,
         name="weights",
     )(energies, update, weights)

time: 59.6 us -> 59.6 us (level)
  Pallas kernels: 14.7 us -> 14.1 us
  transfers between devices with their start and end apart: 3 -> 3, of which waited for: 2 -> 2; matrix products, arithmetic and copies ran while one was open for 0% -> 0% of each run, Pallas kernels for 14% -> 13%
where the time goes in v7:
time: 59.6 us; the launch traced here: 59.2 us
  starting transfers between devices  32.2 us (54%)
  Pallas kernels  14.1 us (24%)
  waiting for transfers between devices  12.2 us (20%)
  between operations  0.7 us (1%)
    all_to_all x1, starting transfers between devices, on_device(): lax.all_to_all(send.reshape(replicas * ROWS, 1, 128), 'dp', 0, 0, tiled=T...  20.4 us
    all_to_all x1, starting transfers between devices, on_device(): lax.all_to_all(energy.reshape(2 * nmp, 1, 128), ('dp', 'mp'), 0, 0, tiled...  9.26 us
    all_to_all x1, waiting for transfers between devices, on_device(): lax.all_to_all(send.reshape(replicas * ROWS, 1, 128), 'dp', 0, 0, tiled=T...  6.5 us
    pallas_call x1, Pallas kernels, on_device(): pl.pallas_call(momentum_kernel, grid=(steps,), in_specs=[tile, tile, whol...  5.83 us
    all_to_all x1, waiting for transfers between devices, on_device(): lax.all_to_all(energy.reshape(2 * nmp, 1, 128), ('dp', 'mp'), 0, 0, tiled...  5.69 us
    pallas_call x1, Pallas kernels, on_device(): pl.pallas_call(send_kernel, in_specs=[hbm] * 5, out_shape=jax.ShapeDtypeS...  3.72 us
    ppermute x1, starting transfers between devices, on_device(): other = lax.ppermute(coef, 'dp', [(p, p ^ 1) for p in range(replicas)])  2.59 us
    pallas_call x1, Pallas kernels, on_device(): pl.pallas_call(inverse_kernel, in_specs=[pl.BlockSpec(memory_space=pltpu....  1.76 us
  transfers between devices with their start and end apart: 3, of which 2 were waited for; matrix products, arithmetic and copies ran while one was open for 0% of the time, Pallas kernels for 13%

profile of v7, /device:TPU:1, one launch (start us, length us, event | category | flops | bytes accessed | tf_op | source)
XLA Modules:
  0.0 59.2 jit_solution(16588778504368985578)
XLA Ops:
  0.6 3.7 %send.1 = f32[1088,128]{1,0:T(8,128)} custom-call(f32[64,4096]{1,0:T(8,128)} %bitcast.18, bf16[64,4096]{1,0:T(8,128)(2,1)} %bitcast.21, s32[4,64]{1,0:T(4,128)} %bitcast.23, s32[1,64]{1,0:T(1,128)} %bitcast.25, bf16[576,256]{1,0:T(8,128)(2,1)} %constant.13.clone.forward_ref.weights_hbm), custom_call_target="tpu_custom_call" | custom-call | tf_op jit(solution)/shard_map/send/pallas_call | solution.py:312
  4.4 20.4 %all-to-all-start = ((f32[1088,1,128]{2,1,0:T(1,128)}), f32[1088,1,128]{2,1,0:T(1,128)S(1)}, u32[]{:S(2)}, u32[]{:S(2)}) async-start(f32[1088,1,128]{2,1,0:T(1,128)} %bitcast.8), calls=%async_computation | async-start | bytes 1114112 | tf_op jit(solution)/shard_map/all_to_all | solution.py:329
  24.7 5.8 %momentum.1._ = f32[64,4096]{1,0:T(8,128)} custom-call(f32[64,4096]{1,0:T(8,128)} %bitcast.19, bf16[64,4096]{1,0:T(8,128)(2,1)} %bitcast.22, s32[4,64]{1,0:T(4,128)} %bitcast.24, s32[1,64]{1,0:T(1,128)} %bitcast.26, bf16[576,256]{1,0:T(8,128)(2,1)} %constant.13.clone.forward_ref.weights_hbm, bf16[576,256]{1,0:T(8,128)(2,1)} %constant.14.clone.inverse_ref), custom_call_target="tpu_custom_call" | custom-call | flops 805306368 | bytes 2621440 | tf_op jit(solution)/shard_map/momentum/pallas_call | solution.py:330
  30.6 6.5 %all-to-all-done = f32[1088,1,128]{2,1,0:T(1,128)S(1)} async-done(((f32[1088,1,128]{2,1,0:T(1,128)}), f32[1088,1,128]{2,1,0:T(1,128)S(1)}, u32[]{:S(2)}, u32[]{:S(2)}) %all-to-all-start) | async-done | bytes 557088 | tf_op jit(solution)/shard_map/all_to_all | solution.py:329
  37.1 0.0 copy-start.1
  37.1 1.6 %scatter.1 = (f32[512,256]{1,0:T(8,128)S(1)}, f32[24,128]{1,0:T(8,128)}) custom-call(f32[1088,128]{1,0:T(8,128)S(1)} %bitcast.16, f32[64,4096]{1,0:T(8,128)} %momentum.1._), custom_call_target="tpu_custom_call" | custom-call | tf_op jit(solution)/shard_map/scatter/pallas_call | solution.py:341
  38.7 2.6 %collective-permute-start = (f32[512,256]{1,0:T(8,128)S(1)}, f32[512,256]{1,0:T(8,128)S(1)}, u32[]{:S(2)}, u32[]{:S(2)}) collective-permute-start(f32[512,256]{1,0:T(8,128)S(1)} %get-tuple-element.5.own_ref), channel_id=1, source_target_pairs={{0,12},{12,0},{24,36},{36,24},{48,60},{60,48},{72,84},{84,72},{96,... | collective-permute-start | bytes 1572872 | tf_op jit(solution)/shard_map/ppermute | solution.py:357
  41.3 9.3 %all-to-all-start.1 = ((f32[24,1,128]{2,1,0:T(1,128)}), f32[24,1,128]{2,1,0:T(1,128)S(1)}, u32[]{:S(2)}, u32[]{:S(2)}) async-start(f32[24,1,128]{2,1,0:T(1,128)} %bitcast.11), calls=%async_computation.1 | async-start | bytes 24576 | tf_op jit(solution)/shard_map/all_to_all | solution.py:355
  50.5 0.0 collective-permute-done.other_ref
  50.5 0.0 copy-done.1
  50.6 0.0 copy-start
  50.6 1.8 %inverse.1.update_ref = f32[64,4096]{1,0:T(8,128)S(1)} custom-call(s32[1]{0:T(128)} %bitcast.13.core_ref, f32[512,256]{1,0:T(8,128)S(1)} %get-tuple-element.5.own_ref, f32[512,256]{1,0:T(8,128)S(1)} %collective-permute-done.other_ref, bf16[576,256]{1,0:T(8,128)(2,1)S(1)} %copy-done.1), custom_call_target="tpu_custom_call" | custom-call | flops 402653184 | bytes 2097152 | tf_op jit(solution)/shard_map/inverse/pallas_call | solution.py:359
  52.3 5.7 %all-to-all-done.1 = f32[24,1,128]{2,1,0:T(1,128)S(1)} async-done(((f32[24,1,128]{2,1,0:T(1,128)}), f32[24,1,128]{2,1,0:T(1,128)S(1)}, u32[]{:S(2)}, u32[]{:S(2)}) %all-to-all-start.1) | async-done | bytes 12320 | tf_op jit(solution)/shard_map/all_to_all | solution.py:355
  58.0 0.0 copy-done
  58.0 1.2 %weights.1 = f32[64,4096]{1,0:T(8,128)} custom-call(f32[24,128]{1,0:T(8,128)S(1)} %bitcast.17, f32[64,4096]{1,0:T(8,128)S(1)} %inverse.1.update_ref, f32[64,4096]{1,0:T(8,128)S(1)} %copy-done), custom_call_target="tpu_custom_call" | custom-call | tf_op jit(solution)/shard_map/weights/pallas_call | solution.py:369
Async XLA Ops:
  4.4 32.7 %all-to-all-start = ((f32[1088,1,128]{2,1,0:T(1,128)}), f32[1088,1,128]{2,1,0:T(1,128)S(1)}, u32[]{:S(2)}, u32[]{:S(2)}) async-start(f32[1088,1,128]{2,1,0:T(1,128)} %bitcast.8), calls=%async_computation | async-start | bytes 1114112 | tf_op jit(solution)/shard_map/all_to_all | solution.py:329
  37.1 13.5 %copy-start.1 = (bf16[576,256]{1,0:T(8,128)(2,1)S(1)}, bf16[576,256]{1,0:T(8,128)(2,1)}, u32[]{:S(2)}) copy-start(bf16[576,256]{1,0:T(8,128)(2,1)} %constant.15.clone.weights_ref) | copy-start | bytes 884740
  38.7 11.9 %collective-permute-start = (f32[512,256]{1,0:T(8,128)S(1)}, f32[512,256]{1,0:T(8,128)S(1)}, u32[]{:S(2)}, u32[]{:S(2)}) collective-permute-start(f32[512,256]{1,0:T(8,128)S(1)} %get-tuple-element.5.own_ref), channel_id=1, source_target_pairs={{0,12},{12,0},{24,36},{36,24},{48,60},{60,48},{72,84},{84,72},{96,... | collective-permute-start | bytes 1572872 | tf_op jit(solution)/shard_map/ppermute | solution.py:357
  41.3 16.8 %all-to-all-start.1 = ((f32[24,1,128]{2,1,0:T(1,128)}), f32[24,1,128]{2,1,0:T(1,128)S(1)}, u32[]{:S(2)}, u32[]{:S(2)}) async-start(f32[24,1,128]{2,1,0:T(1,128)} %bitcast.11), calls=%async_computation.1 | async-start | bytes 24576 | tf_op jit(solution)/shard_map/all_to_all | solution.py:355
  50.6 7.5 %copy-start = (f32[64,4096]{1,0:T(8,128)S(1)}, f32[64,4096]{1,0:T(8,128)}, u32[]{:S(2)}) copy-start(f32[64,4096]{1,0:T(8,128)} %weights_ref.2) | copy-start | bytes 3145732

commit v8 on v7

--- a/solution.py
+++ b/solution.py
@@ -78,7 +78,8 @@
 def times_right(x, weights):
     high, low = split(x)
     top = weights[GROUP : GROUP + QUAD]
-    return dot(high, top) + (dot(low, top) + dot(high, weights[GROUP + QUAD :]))
+    both = dot(jnp.concatenate([high, low], axis=0), top)
+    return both[: x.shape[0]] + (both[x.shape[0] :] + dot(high, weights[GROUP + QUAD :]))
 
 
 def flag(cond):

time: 59.6 us -> 59.6 us (level)
  no operation moved by 1% of the time
where the time goes in v8:
time: 59.6 us; the launch traced here: 59.2 us
  starting transfers between devices  32.2 us (54%)
  Pallas kernels  14.2 us (24%)
  waiting for transfers between devices  12.1 us (20%)
  between operations  0.7 us (1%)
    all_to_all x1, starting transfers between devices, on_device(): lax.all_to_all(send.reshape(replicas * ROWS, 1, 128), 'dp', 0, 0, tiled=T...  20.3 us
    all_to_all x1, starting transfers between devices, on_device(): lax.all_to_all(energy.reshape(2 * nmp, 1, 128), ('dp', 'mp'), 0, 0, tiled...  9.26 us
    all_to_all x1, waiting for transfers between devices, on_device(): lax.all_to_all(send.reshape(replicas * ROWS, 1, 128), 'dp', 0, 0, tiled=T...  6.39 us
    pallas_call x1, Pallas kernels, on_device(): pl.pallas_call(momentum_kernel, grid=(steps,), in_specs=[tile, tile, whol...  5.95 us
    all_to_all x1, waiting for transfers between devices, on_device(): lax.all_to_all(energy.reshape(2 * nmp, 1, 128), ('dp', 'mp'), 0, 0, tiled...  5.68 us
    pallas_call x1, Pallas kernels, on_device(): pl.pallas_call(send_kernel, in_specs=[hbm] * 5, out_shape=jax.ShapeDtypeS...  3.72 us
    ppermute x1, starting transfers between devices, on_device(): other = lax.ppermute(coef, 'dp', [(p, p ^ 1) for p in range(replicas)])  2.59 us
    pallas_call x1, Pallas kernels, on_device(): pl.pallas_call(inverse_kernel, in_specs=[pl.BlockSpec(memory_space=pltpu....  1.76 us
  transfers between devices with their start and end apart: 3, of which 2 were waited for; matrix products, arithmetic and copies ran while one was open for 0% of the time, Pallas kernels for 13%

profile of v8, /device:TPU:1, one launch (start us, length us, event | category | flops | bytes accessed | tf_op | source)
XLA Modules:
  0.0 59.2 jit_solution(7613234299952661851)
XLA Ops:
  0.6 3.7 %send.1 = f32[1088,128]{1,0:T(8,128)} custom-call(f32[64,4096]{1,0:T(8,128)} %bitcast.18, bf16[64,4096]{1,0:T(8,128)(2,1)} %bitcast.21, s32[4,64]{1,0:T(4,128)} %bitcast.23, s32[1,64]{1,0:T(1,128)} %bitcast.25, bf16[576,256]{1,0:T(8,128)(2,1)} %constant.13.clone.forward_ref.weights_hbm), custom_call_target="tpu_custom_call" | custom-call | tf_op jit(solution)/shard_map/send/pallas_call | solution.py:313
  4.4 20.3 %all-to-all-start = ((f32[1088,1,128]{2,1,0:T(1,128)}), f32[1088,1,128]{2,1,0:T(1,128)S(1)}, u32[]{:S(2)}, u32[]{:S(2)}) async-start(f32[1088,1,128]{2,1,0:T(1,128)} %bitcast.8), calls=%async_computation | async-start | bytes 1114112 | tf_op jit(solution)/shard_map/all_to_all | solution.py:330
  24.7 5.9 %momentum.1._ = f32[64,4096]{1,0:T(8,128)} custom-call(f32[64,4096]{1,0:T(8,128)} %bitcast.19, bf16[64,4096]{1,0:T(8,128)(2,1)} %bitcast.22, s32[4,64]{1,0:T(4,128)} %bitcast.24, s32[1,64]{1,0:T(1,128)} %bitcast.26, bf16[576,256]{1,0:T(8,128)(2,1)} %constant.13.clone.forward_ref.weights_hbm, bf16[576,256]{1,0:T(8,128)(2,1)} %constant.14.clone.inverse_ref), custom_call_target="tpu_custom_call" | custom-call | flops 805306368 | bytes 2621440 | tf_op jit(solution)/shard_map/momentum/pallas_call | solution.py:331
  30.7 6.4 %all-to-all-done = f32[1088,1,128]{2,1,0:T(1,128)S(1)} async-done(((f32[1088,1,128]{2,1,0:T(1,128)}), f32[1088,1,128]{2,1,0:T(1,128)S(1)}, u32[]{:S(2)}, u32[]{:S(2)}) %all-to-all-start) | async-done | bytes 557088 | tf_op jit(solution)/shard_map/all_to_all | solution.py:330
  37.1 0.0 copy-start.1
  37.1 1.6 %scatter.1 = (f32[512,256]{1,0:T(8,128)S(1)}, f32[24,128]{1,0:T(8,128)}) custom-call(f32[1088,128]{1,0:T(8,128)S(1)} %bitcast.16, f32[64,4096]{1,0:T(8,128)} %momentum.1._), custom_call_target="tpu_custom_call" | custom-call | tf_op jit(solution)/shard_map/scatter/pallas_call | solution.py:342
  38.7 2.6 %collective-permute-start = (f32[512,256]{1,0:T(8,128)S(1)}, f32[512,256]{1,0:T(8,128)S(1)}, u32[]{:S(2)}, u32[]{:S(2)}) collective-permute-start(f32[512,256]{1,0:T(8,128)S(1)} %get-tuple-element.5.own_ref), channel_id=1, source_target_pairs={{0,12},{12,0},{24,36},{36,24},{48,60},{60,48},{72,84},{84,72},{96,... | collective-permute-start | bytes 1572872 | tf_op jit(solution)/shard_map/ppermute | solution.py:358
  41.3 9.3 %all-to-all-start.1 = ((f32[24,1,128]{2,1,0:T(1,128)}), f32[24,1,128]{2,1,0:T(1,128)S(1)}, u32[]{:S(2)}, u32[]{:S(2)}) async-start(f32[24,1,128]{2,1,0:T(1,128)} %bitcast.11), calls=%async_computation.1 | async-start | bytes 24576 | tf_op jit(solution)/shard_map/all_to_all | solution.py:356
  50.5 0.0 collective-permute-done.other_ref
  50.5 0.0 copy-done.1
  50.6 0.0 copy-start
  50.6 1.8 %inverse.1.update_ref = f32[64,4096]{1,0:T(8,128)S(1)} custom-call(s32[1]{0:T(128)} %bitcast.13.core_ref, f32[512,256]{1,0:T(8,128)S(1)} %get-tuple-element.5.own_ref, f32[512,256]{1,0:T(8,128)S(1)} %collective-permute-done.other_ref, bf16[576,256]{1,0:T(8,128)(2,1)S(1)} %copy-done.1), custom_call_target="tpu_custom_call" | custom-call | flops 402653184 | bytes 2097152 | tf_op jit(solution)/shard_map/inverse/pallas_call | solution.py:360
  52.3 5.7 %all-to-all-done.1 = f32[24,1,128]{2,1,0:T(1,128)S(1)} async-done(((f32[24,1,128]{2,1,0:T(1,128)}), f32[24,1,128]{2,1,0:T(1,128)S(1)}, u32[]{:S(2)}, u32[]{:S(2)}) %all-to-all-start.1) | async-done | bytes 12320 | tf_op jit(solution)/shard_map/all_to_all | solution.py:356
  58.0 0.0 copy-done
  58.0 1.2 %weights.1 = f32[64,4096]{1,0:T(8,128)} custom-call(f32[24,128]{1,0:T(8,128)S(1)} %bitcast.17, f32[64,4096]{1,0:T(8,128)S(1)} %inverse.1.update_ref, f32[64,4096]{1,0:T(8,128)S(1)} %copy-done), custom_call_target="tpu_custom_call" | custom-call | tf_op jit(solution)/shard_map/weights/pallas_call | solution.py:370
Async XLA Ops:
  4.4 32.7 %all-to-all-start = ((f32[1088,1,128]{2,1,0:T(1,128)}), f32[1088,1,128]{2,1,0:T(1,128)S(1)}, u32[]{:S(2)}, u32[]{:S(2)}) async-start(f32[1088,1,128]{2,1,0:T(1,128)} %bitcast.8), calls=%async_computation | async-start | bytes 1114112 | tf_op jit(solution)/shard_map/all_to_all | solution.py:330
  37.1 13.5 %copy-start.1 = (bf16[576,256]{1,0:T(8,128)(2,1)S(1)}, bf16[576,256]{1,0:T(8,128)(2,1)}, u32[]{:S(2)}) copy-start(bf16[576,256]{1,0:T(8,128)(2,1)} %constant.15.clone.weights_ref) | copy-start | bytes 884740
  38.7 11.9 %collective-permute-start = (f32[512,256]{1,0:T(8,128)S(1)}, f32[512,256]{1,0:T(8,128)S(1)}, u32[]{:S(2)}, u32[]{:S(2)}) collective-permute-start(f32[512,256]{1,0:T(8,128)S(1)} %get-tuple-element.5.own_ref), channel_id=1, source_target_pairs={{0,12},{12,0},{24,36},{36,24},{48,60},{60,48},{72,84},{84,72},{96,... | collective-permute-start | bytes 1572872 | tf_op jit(solution)/shard_map/ppermute | solution.py:358
  41.3 16.8 %all-to-all-start.1 = ((f32[24,1,128]{2,1,0:T(1,128)}), f32[24,1,128]{2,1,0:T(1,128)S(1)}, u32[]{:S(2)}, u32[]{:S(2)}) async-start(f32[24,1,128]{2,1,0:T(1,128)} %bitcast.11), calls=%async_computation.1 | async-start | bytes 24576 | tf_op jit(solution)/shard_map/all_to_all | solution.py:356
  50.6 7.5 %copy-start = (f32[64,4096]{1,0:T(8,128)S(1)}, f32[64,4096]{1,0:T(8,128)}, u32[]{:S(2)}) copy-start(f32[64,4096]{1,0:T(8,128)} %weights_ref.2) | copy-start | bytes 3145732
